TPU v7x, 128 devices: a whole 4x4x4 slice. The times are simulated.
128 devices in a mesh: seq: 8 (over y, core), head: 16 (over z, x).
Axes of the slice: x: 4, y: 4, z: 4, core: 2. Of those that a mesh axis runs over, the one named last changes fastest.
Arguments:
- layer_input: bfloat16 [16384, 1024], P(('seq', 'head')), may hold values from -6 to 6
- second_start: int32 [8], P('seq'), may hold values from 1921 to 2048, as said below
- mixer_gain: bfloat16 [1024], replicated, may hold values from 0.099609375 to 1.8984375
- w_query: bfloat16 [1024, 1024], replicated, may hold values from -0.1875 to 0.1875
- w_query_rope: bfloat16 [1024, 512], replicated, may hold values from -0.1875 to 0.1875
- w_latent: bfloat16 [1024, 512], replicated, may hold values from -0.1875 to 0.1875
- w_key_rope: bfloat16 [1024, 32], replicated, may hold values from -0.1875 to 0.1875
- w_key_up: bfloat16 [2, 256, 512], replicated, may hold values from -0.375 to 0.375
- w_value_up: bfloat16 [2, 256, 512], replicated, may hold values from -0.375 to 0.375
- w_out: bfloat16 [1024, 1024], replicated, may hold values from -0.75 to 0.75
- feed_gain: bfloat16 [1024], replicated, may hold values from 0.099609375 to 1.8984375
- w_gate: bfloat16 [1024, 2816], replicated, may hold values from -0.1875 to 0.1875
- w_up: bfloat16 [1024, 2816], replicated, may hold values from -0.1875 to 0.1875
- w_down: bfloat16 [2816, 1024], replicated, may hold values from -0.109375 to 0.109375
- cotangent: bfloat16 [16384, 1024], P(('seq', 'head')), may hold values from -6 to 6
Outputs:
- output: bfloat16 [16384, 1024], P(('seq', 'head'))
- grad_input: float32 [16384, 1024], P(('seq', 'head'))
- grad_mixer_gain: float32 [1024], P(('seq', 'head'))
- grad_w_query: float32 [1024, 1024], P(('seq', 'head'))
- grad_w_query_rope: float32 [1024, 512], P(('seq', 'head'))
- grad_w_latent: float32 [1024, 512], P(('seq', 'head'))
- grad_w_key_rope: float32 [1024, 32], P(('seq', 'head'))
- grad_w_key_up: float32 [2, 256, 512], P(None, None, ('seq', 'head'))
- grad_w_value_up: float32 [2, 256, 512], P(None, None, ('seq', 'head'))
- grad_w_out: float32 [1024, 1024], P(('seq', 'head'))
- grad_feed_gain: float32 [1024], P(('seq', 'head'))
- grad_w_gate: float32 [1024, 2816], P(('seq', 'head'))
- grad_w_up: float32 [1024, 2816], P(('seq', 'head'))
- grad_w_down: float32 [2816, 1024], P(None, ('seq', 'head'))
Inputs may be any that keep to these rules, and one draw needn't show every extreme that they name: Each group's first sequence reaches into its last 128 tokens: second_start is 2048 (one sequence) or lies within the group's last 128 tokens; both ends of the range occur in every draw.
All inputs are finite; a program needn't handle non-finite values.
Results may differ from a plain program's by a relative error of at most 0.015.
Values may be sent and summed in bfloat16 or wider, within the bound.
A program may use at most 192 MiB of HBM per device.

v0:
```python
import math

import jax
import jax.numpy as jnp
import numpy as np
from jax import lax
from jax.sharding import PartitionSpec as P

HEADS = 16
HEAD_DIM = 64
ROPE = 32
LATENT = 256
LATENT_HEADS = 2


epsilon = 1e-06


def for_sending(x):

    def short(part):
        return part.astype(jnp.bfloat16) if part.dtype == jnp.float32 else part

    return jax.tree.map(short, x)


def across(left, right):
    return lax.dot_general(
        left, right, (((0,), (0,)), ((), ())), preferred_element_type=jnp.float32
    )


def against(left, right):
    return lax.dot_general(
        left, right, (((1,), (1,)), ((), ())), preferred_element_type=jnp.float32
    )


def turning(positions, width):
    half = width // 2
    freqs = 10000.0 ** (-jnp.arange(half, dtype=jnp.float32) * 2.0 / width)
    angles = positions.astype(jnp.float32)[:, None] * freqs[None, :]
    return (jnp.cos(angles), jnp.sin(angles))


def rotate(values, cosine, sine):
    half = values.shape[-1] // 2
    first = values[..., :half]
    second = values[..., half:]
    return jnp.concatenate([first * cosine - second * sine, first * sine + second * cosine], -1)


def normalize(values, gain):
    inverse = lax.rsqrt(jnp.mean(values * values, -1, keepdims=True) + epsilon)
    return (values * inverse * gain, inverse)


def norm_back(values, inverse, gain, upstream):
    scaled = upstream * gain
    grad_values = inverse * scaled - values * (inverse * inverse * inverse) * jnp.mean(
        values * scaled, -1, keepdims=True
    )
    grad_gain = jnp.sum(upstream * values * inverse, 0)
    return (grad_values, grad_gain)


def body(
    layer_input,
    second_start,
    mixer_gain,
    w_query,
    w_query_rope,
    w_latent,
    w_key_rope,
    w_key_up,
    w_value_up,
    w_out,
    feed_gain,
    w_gate,
    w_up,
    w_down,
    cotangent,
):
    local_rows = layer_input.shape[0]
    head_devs = lax.axis_size("head")
    per_device = HEADS // head_devs
    share = HEADS // LATENT_HEADS
    group_rows = local_rows * head_devs
    block_rows = min(512, group_rows)
    blocks = group_rows // block_rows
    scale = 1.0 / math.sqrt(HEAD_DIM + ROPE)
    query_width = per_device * HEAD_DIM
    rope_width = per_device * ROPE
    mine = lax.axis_index("head")
    boundary = second_start[0]
    inputs32 = layer_input.astype(jnp.float32)
    gain_one = mixer_gain.astype(jnp.float32)
    gain_two = feed_gain.astype(jnp.float32)
    hidden_one, inverse_one = normalize(inputs32, gain_one)
    normed_one = hidden_one.astype(jnp.bfloat16)
    local_index = mine * local_rows + jnp.arange(local_rows, dtype=jnp.int32)
    local_pos = local_index - jnp.where(local_index >= boundary, boundary, 0)
    cosine, sine = turning(local_pos, ROPE)
    query = jnp.dot(normed_one, w_query, preferred_element_type=jnp.float32).astype(jnp.bfloat16)
    turned = jnp.dot(normed_one, w_query_rope, preferred_element_type=jnp.float32).reshape(
        local_rows, HEADS, ROPE
    )
    query_rope = rotate(turned, cosine[:, None], sine[:, None]).astype(jnp.bfloat16)
    latent = jnp.dot(normed_one, w_latent, preferred_element_type=jnp.float32).astype(jnp.bfloat16)
    key_rope = rotate(
        jnp.dot(normed_one, w_key_rope, preferred_element_type=jnp.float32), cosine, sine
    ).astype(jnp.bfloat16)
    latent_three = latent.reshape(local_rows, LATENT_HEADS, LATENT)
    rope_spread = jnp.broadcast_to(key_rope[:, None], (local_rows, head_devs, ROPE))
    first_head = mine * per_device
    latent_index = first_head // share
    column = first_head % share * HEAD_DIM
    anchor = jnp.zeros((), jnp.int32)
    key_up = lax.dynamic_slice(w_key_up, (latent_index, anchor, column), (1, LATENT, query_width))[
        0
    ]
    value_up = lax.dynamic_slice(
        w_value_up, (latent_index, anchor, column), (1, LATENT, query_width)
    )[0]
    query_send = jnp.concatenate(
        [query.reshape(local_rows, head_devs, query_width), query_rope], -1
    )
    targets = np.arange(head_devs) * per_device // share
    latent_send = jnp.concatenate([latent_three[:, targets], rope_spread], -1)
    got_query, got_latent = (
        lax.all_to_all(query_send, "head", split_axis=1, concat_axis=0, tiled=True),
        lax.all_to_all(latent_send, "head", split_axis=1, concat_axis=0, tiled=True),
    )
    head_query = got_query[:, 0, :query_width].reshape(group_rows, per_device, HEAD_DIM)
    head_query_rope = got_query[:, 0, query_width:].reshape(group_rows, per_device, ROPE)
    group_latent = got_latent[:, 0, :LATENT]
    group_key_rope = got_latent[:, 0, LATENT:]
    head_key = (
        jnp.dot(group_latent, key_up, preferred_element_type=jnp.float32)
        .astype(jnp.bfloat16)
        .reshape(group_rows, per_device, HEAD_DIM)
    )
    head_value = (
        jnp.dot(group_latent, value_up, preferred_element_type=jnp.float32)
        .astype(jnp.bfloat16)
        .reshape(group_rows, per_device, HEAD_DIM)
    )
    positions = jnp.arange(group_rows, dtype=jnp.int32)
    later = positions >= boundary

    def scores(start):
        rows = start + jnp.arange(block_rows, dtype=jnp.int32)
        block_query = lax.dynamic_slice_in_dim(head_query, start, block_rows, 0)
        block_rope = lax.dynamic_slice_in_dim(head_query_rope, start, block_rows, 0)
        raw = jnp.einsum("bhd,khd->hbk", block_query, head_key, preferred_element_type=jnp.float32)
        raw = (
            raw
            + jnp.einsum(
                "bhr,kr->hbk", block_rope, group_key_rope, preferred_element_type=jnp.float32
            )
        ) * scale
        allowed = (positions[None, :] <= rows[:, None]) & (
            later[None, :] == (rows[:, None] >= boundary)
        )
        return (jnp.where(allowed[None], raw, -1e30), block_query, block_rope)

    def forward_block(start):
        masked, unused_query, unused_rope = scores(start)
        top = jnp.max(masked, -1, keepdims=True)
        weights = jnp.exp(masked - top)
        total = jnp.sum(weights, -1, keepdims=True)
        probs = (weights / total).astype(jnp.bfloat16)
        result = jnp.einsum(
            "hbk,khd->bhd", probs, head_value, preferred_element_type=jnp.float32
        ).astype(jnp.bfloat16)
        return (result, (top + jnp.log(total))[..., 0])

    starts = jnp.arange(blocks, dtype=jnp.int32) * block_rows
    head_out, log_totals = lax.map(forward_block, starts)
    returned = lax.all_to_all(
        for_sending(head_out.reshape(group_rows, 1, query_width)),
        "head",
        split_axis=0,
        concat_axis=1,
        tiled=True,
    )
    attended = returned.reshape(local_rows, HEADS * HEAD_DIM)
    middle = inputs32 + jnp.dot(attended, w_out, preferred_element_type=jnp.float32)
    hidden_two, inverse_two = normalize(middle, gain_two)
    normed_two = hidden_two.astype(jnp.bfloat16)
    gate = jnp.dot(normed_two, w_gate, preferred_element_type=jnp.float32)
    upward = jnp.dot(normed_two, w_up, preferred_element_type=jnp.float32)
    sigma = jax.nn.sigmoid(gate)
    swish = gate * sigma
    activated = (swish * upward).astype(jnp.bfloat16)
    output = (middle + jnp.dot(activated, w_down, preferred_element_type=jnp.float32)).astype(
        jnp.bfloat16
    )
    grad_down = across(activated, cotangent)
    grad_act = against(cotangent, w_down)
    grad_gate = (grad_act * upward * sigma * (1.0 + gate * (1.0 - sigma))).astype(jnp.bfloat16)
    grad_upward = (grad_act * swish).astype(jnp.bfloat16)
    grad_wgate = across(normed_two, grad_gate)
    grad_wup = across(normed_two, grad_upward)
    grad_two = against(grad_gate, w_gate) + against(grad_upward, w_up)
    grad_mid_norm, grad_gain_two = norm_back(middle, inverse_two, gain_two, grad_two)
    grad_middle = cotangent.astype(jnp.float32) + grad_mid_norm
    grad_branch = grad_middle.astype(jnp.bfloat16)
    grad_wout = across(attended, grad_branch)
    grad_attended = against(grad_branch, w_out).astype(jnp.bfloat16)
    head_grad = lax.all_to_all(
        grad_attended.reshape(local_rows, head_devs, query_width),
        "head",
        split_axis=1,
        concat_axis=0,
        tiled=True,
    )

    def backward_block(carry, inputs):
        grad_key, grad_value, grad_key_rope = carry
        start, block_log = inputs
        masked, block_query, block_rope = scores(start)
        probs = jnp.exp(masked - block_log[..., None])
        block_grad = lax.dynamic_slice_in_dim(head_grad, start, block_rows, 0)
        grad_value = grad_value + jnp.einsum(
            "hbk,bhd->khd",
            probs.astype(jnp.bfloat16),
            block_grad,
            preferred_element_type=jnp.float32,
        )
        grad_probs = jnp.einsum(
            "bhd,khd->hbk", block_grad, head_value, preferred_element_type=jnp.float32
        )
        inner = jnp.sum(probs * grad_probs, -1, keepdims=True)
        grad_scores = (probs * (grad_probs - inner)).astype(jnp.bfloat16)
        grad_query = (
            jnp.einsum("hbk,khd->bhd", grad_scores, head_key, preferred_element_type=jnp.float32)
            * scale
        ).astype(jnp.bfloat16)
        grad_turned = (
            jnp.einsum(
                "hbk,kr->bhr", grad_scores, group_key_rope, preferred_element_type=jnp.float32
            )
            * scale
        ).astype(jnp.bfloat16)
        grad_key = (
            grad_key
            + jnp.einsum(
                "hbk,bhd->khd", grad_scores, block_query, preferred_element_type=jnp.float32
            )
            * scale
        )
        grad_key_rope = (
            grad_key_rope
            + jnp.einsum("hbk,bhr->kr", grad_scores, block_rope, preferred_element_type=jnp.float32)
            * scale
        )
        return ((grad_key, grad_value, grad_key_rope), (grad_query, grad_turned))

    initial = (
        jnp.zeros((group_rows, per_device, HEAD_DIM), jnp.float32),
        jnp.zeros((group_rows, per_device, HEAD_DIM), jnp.float32),
        jnp.zeros((group_rows, ROPE), jnp.float32),
    )
    sums_kept, per_block = lax.scan(backward_block, initial, (starts, log_totals))
    key_grad_low = sums_kept[0].astype(jnp.bfloat16).reshape(group_rows, query_width)
    value_grad_low = sums_kept[1].astype(jnp.bfloat16).reshape(group_rows, query_width)
    query_back = jnp.concatenate(
        [
            per_block[0].reshape(group_rows, query_width),
            per_block[1].reshape(group_rows, rope_width),
        ],
        -1,
    )[:, None]
    got_qgrad = lax.all_to_all(query_back, "head", split_axis=0, concat_axis=1, tiled=True)
    grad_kup = lax.dynamic_update_slice(
        jnp.zeros(w_key_up.shape, jnp.float32),
        across(group_latent, key_grad_low)[None],
        (latent_index, anchor, column),
    )
    grad_vup = lax.dynamic_update_slice(
        jnp.zeros(w_value_up.shape, jnp.float32),
        across(group_latent, value_grad_low)[None],
        (latent_index, anchor, column),
    )
    grad_group_latent = against(key_grad_low, key_up) + against(value_grad_low, value_up)
    latent_back = jnp.concatenate([grad_group_latent, sums_kept[2]], -1)[:, None]
    got_lgrad = lax.all_to_all(
        latent_back.astype(jnp.bfloat16), "head", split_axis=0, concat_axis=1, tiled=True
    ).astype(latent_back.dtype)
    grouped = jnp.sum(
        got_lgrad.reshape(local_rows, LATENT_HEADS, head_devs // LATENT_HEADS, LATENT + ROPE), 2
    )
    grad_latent = (
        grouped[:, :, :LATENT].reshape(local_rows, LATENT_HEADS * LATENT).astype(jnp.bfloat16)
    )
    grad_kturn = lax.optimization_barrier(
        jnp.sum(grouped[:, :, LATENT:], 1).astype(jnp.bfloat16)
    ).astype(jnp.float32)
    grad_query_all = got_qgrad[:, :, :query_width].reshape(local_rows, HEADS * HEAD_DIM)
    grad_qturn = got_qgrad[:, :, query_width:].reshape(local_rows, HEADS, ROPE).astype(jnp.float32)
    grad_qrope = (
        rotate(grad_qturn, cosine[:, None], -sine[:, None])
        .astype(jnp.bfloat16)
        .reshape(local_rows, HEADS * ROPE)
    )
    grad_kpre = rotate(grad_kturn, cosine, -sine).astype(jnp.bfloat16)
    grad_wq = across(normed_one, grad_query_all)
    grad_wqr = across(normed_one, grad_qrope)
    grad_wlat = across(normed_one, grad_latent)
    grad_wkr = across(normed_one, grad_kpre)
    grad_one = (
        against(grad_query_all, w_query)
        + against(grad_qrope, w_query_rope)
        + against(grad_latent, w_latent)
        + against(grad_kpre, w_key_rope)
    )
    grad_in_norm, grad_gain_one = norm_back(inputs32, inverse_one, gain_one, grad_one)
    grad_input = grad_middle + grad_in_norm
    summed = (
        lax.psum_scatter(grad_gain_one, ("seq", "head"), scatter_dimension=0, tiled=True),
        lax.psum_scatter(grad_wq, ("seq", "head"), scatter_dimension=0, tiled=True),
        lax.psum_scatter(grad_wqr, ("seq", "head"), scatter_dimension=0, tiled=True),
        lax.psum_scatter(grad_wlat, ("seq", "head"), scatter_dimension=0, tiled=True),
        lax.psum_scatter(grad_wkr, ("seq", "head"), scatter_dimension=0, tiled=True),
        lax.psum_scatter(grad_kup, ("seq", "head"), scatter_dimension=2, tiled=True),
        lax.psum_scatter(grad_vup, ("seq", "head"), scatter_dimension=2, tiled=True),
        lax.psum_scatter(grad_wout, ("seq", "head"), scatter_dimension=0, tiled=True),
        lax.psum_scatter(grad_gain_two, ("seq", "head"), scatter_dimension=0, tiled=True),
        lax.psum_scatter(grad_wgate, ("seq", "head"), scatter_dimension=0, tiled=True),
        lax.psum_scatter(grad_wup, ("seq", "head"), scatter_dimension=0, tiled=True),
        lax.psum_scatter(grad_down, ("seq", "head"), scatter_dimension=1, tiled=True),
    )
    return (
        output,
        grad_input,
        summed[0],
        summed[1],
        summed[2],
        summed[3],
        summed[4],
        summed[5],
        summed[6],
        summed[7],
        summed[8],
        summed[9],
        summed[10],
        summed[11],
    )


def solution(mesh):
    in_specs = (
        P(("seq", "head"), None),
        P("seq"),
        P(),
        P(),
        P(),
        P(),
        P(),
        P(),
        P(),
        P(),
        P(),
        P(),
        P(),
        P(),
        P(("seq", "head"), None),
    )
    out_specs = (
        P(("seq", "head"), None),
        P(("seq", "head"), None),
        P(("seq", "head")),
        P(("seq", "head"), None),
        P(("seq", "head"), None),
        P(("seq", "head"), None),
        P(("seq", "head"), None),
        P(None, None, ("seq", "head")),
        P(None, None, ("seq", "head")),
        P(("seq", "head"), None),
        P(("seq", "head")),
        P(("seq", "head"), None),
        P(("seq", "head"), None),
        P(None, ("seq", "head")),
    )
    return jax.shard_map(body, mesh=mesh, in_specs=in_specs, out_specs=out_specs, check_vma=False)
```

profile of v0, /device:TPU:0, one launch (start us, length us, event | category | flops | bytes accessed | tf_op | source)
XLA Modules:
  0.0 5038.3 jit_solution(7657063942970166994)
XLA Ops:
  23.0 8.0 all-to-all-start
  47.6 16.6 all-to-all-done.1
  69.7 44.2 while.35
  120.5 13.4 reduce.3
  139.9 8.6 all-to-all-done.2
  176.0 8.6 all-to-all-done.3
  186.1 86.9 %while.36 = (s32[]{:T(128)}, f32[2048,1,64]{0,2,1:T(8,128)}, f32[2048,1,64]{0,2,1:T(8,128)}, f32[2048,32]{0,1:T(8,128)}, bf16[4,512,1,64]{1,3,2,0:T(8,128)(2,1)}...) while((s32[]{:T(128)}, f32[2048,1,64]{0,2,1:T(8,128)}, ...), condition=%wide.region_9.10_spmd.clone.clone.clone, body=%wide.region_7.9_spmd.clone.clone.clone.sunk | while | flops 887000064 | bytes 71617960 | solution.py:265
  295.8 8.7 all-to-all-done.5
  308.2 10.6 reshape.617
  318.8 6.8 convert_bitcast_fusion
  325.6 5.7 copy.94
  348.0 6.0 fusion.156
  355.1 5.9 fusion.157
  362.2 5.9 fusion.158
  369.1 4.5 fusion.81
  376.8 65.5 %all-reduce.5 = (f32[1024]{0:T(1024)S(1)}, f32[1024]{0:T(1024)S(1)}) all-reduce(f32[1024]{0:T(1024)S(1)} %get-tuple-element.405, f32[1024]{0:T(1024)S(1)} %copy-done.43), channel_id=2, replica_groups=mesh['seq'=8,'head'=16] {'seq','head'}, use_global_device_ids=true, to_apply=%region_14.15.clone | all-reduce | flops 2048 | bytes 16384
  445.8 43.3 all-reduce.9.cloned.1.call-done
  491.7 639.8 %reduce-scatter.12.cloned.1.call-done = f32[8,512]{1,0:T(8,128)} async-done(((f32[1024,512]{1,0:T(8,128)}), f32[8,512]{1,0:T(8,128)}) %reduce-scatter.12.cloned.1.call-update) | async-done | bytes 16400 | tf_op jit(solution)/shard_map/reduce_scatter | solution.py:323
  1131.5 637.1 %reduce-scatter.14.cloned.1.call-done = f32[8,512]{1,0:T(8,128)} async-done(((f32[1024,512]{1,0:T(8,128)}), f32[8,512]{1,0:T(8,128)}) %reduce-scatter.14.cloned.1.call-update) | async-done | bytes 16400 | tf_op jit(solution)/shard_map/reduce_scatter | solution.py:324
  1768.6 640.8 %reduce-scatter.16.cloned.1.call-done = f32[8,1024]{1,0:T(8,128)} async-done(((f32[1024,1024]{1,0:T(8,128)}), f32[8,1024]{1,0:T(8,128)}) %reduce-scatter.16.cloned.1.call-update) | async-done | bytes 32784 | tf_op jit(solution)/shard_map/reduce_scatter | solution.py:328
  2409.4 640.7 %reduce-scatter.10.cloned.1.call-done = f32[8,1024]{1,0:T(8,128)} async-done(((f32[1024,1024]{1,0:T(8,128)}), f32[8,1024]{1,0:T(8,128)}) %reduce-scatter.10.cloned.1.call-update) | async-done | bytes 32784 | tf_op jit(solution)/shard_map/reduce_scatter | solution.py:322
  3050.2 660.4 %reduce-scatter.18.cloned.1.call-done = f32[8,2816]{1,0:T(8,128)} async-done(((f32[1024,2816]{1,0:T(8,128)}), f32[8,2816]{1,0:T(8,128)}) %reduce-scatter.18.cloned.1.call-update) | async-done | bytes 90128 | tf_op jit(solution)/shard_map/reduce_scatter | solution.py:330
  3710.5 660.5 %reduce-scatter.20.cloned.1.call-done = f32[8,2816]{1,0:T(8,128)} async-done(((f32[1024,2816]{1,0:T(8,128)}), f32[8,2816]{1,0:T(8,128)}) %reduce-scatter.20.cloned.1.call-update) | async-done | bytes 90128 | tf_op jit(solution)/shard_map/reduce_scatter | solution.py:331
  4371.1 660.1 %reduce-scatter.22.cloned.1.call-done = f32[2816,8]{0,1:T(8,128)} async-done(((f32[2816,1024]{0,1:T(8,128)}), f32[2816,8]{0,1:T(8,128)}) %reduce-scatter.22.cloned.1.call-update) | async-done | bytes 90128 | tf_op jit(solution)/shard_map/reduce_scatter | solution.py:332
  (373 shorter events, 248.9 us)
Async XLA Ops:
  7.2 145.6 %copy-start = (bf16[1024,1024]{1,0:T(8,128)(2,1)S(1)}, bf16[1024,1024]{1,0:T(8,128)(2,1)}, u32[]{:S(2)}) copy-start(bf16[1024,1024]{1,0:T(8,128)(2,1)} %param.30) | copy-start | bytes 6291460
  8.1 23.0 copy-start.34
  9.8 21.3 copy-start.40
  14.3 16.8 copy-start.19
  23.0 18.2 all-to-all-start
  41.2 23.0 all-to-all-start.1
  113.9 22.2 copy-start.17
  113.9 22.2 copy-start.49
  115.9 23.9 copy-start.48
  136.0 12.4 all-to-all-start.2
  168.6 17.5 copy-start.50
  171.9 12.6 all-to-all-start.3
  284.1 20.3 all-to-all-start.5
  295.8 23.0 copy-start.21
  304.4 30.7 all-to-all-start.4
  308.0 181.1 %all-reduce.9.cloned.1.call-start = ((), (), s32[]{:S(2)}) async-start(), calls=%async_computation.20 | async-start | bytes 5242880
  335.1 796.4 %reduce-scatter.12.cloned.1.call-start = ((), (), s32[]{:S(2)}) async-start(), calls=%async_computation.14 | async-start | bytes 2113536 | tf_op jit(solution)/shard_map/reduce_scatter | solution.py:323
  338.2 1430.4 %reduce-scatter.14.cloned.1.call-start = ((), (), s32[]{:S(2)}) async-start(), calls=%async_computation.15 | async-start | bytes 2113536 | tf_op jit(solution)/shard_map/reduce_scatter | solution.py:324
  341.3 2068.1 %reduce-scatter.16.cloned.1.call-start = ((), (), s32[]{:S(2)}) async-start(), calls=%async_computation.16 | async-start | bytes 4227072 | tf_op jit(solution)/shard_map/reduce_scatter | solution.py:328
  344.1 2706.1 %reduce-scatter.10.cloned.1.call-start = ((), (), s32[]{:S(2)}) async-start(), calls=%async_computation.13 | async-start | bytes 4227072 | tf_op jit(solution)/shard_map/reduce_scatter | solution.py:322
  346.9 3363.6 %reduce-scatter.18.cloned.1.call-start = ((), (), s32[]{:S(2)}) async-start(), calls=%async_computation.17 | async-start | bytes 11624448 | tf_op jit(solution)/shard_map/reduce_scatter | solution.py:330
  354.0 4017.1 %reduce-scatter.20.cloned.1.call-start = ((), (), s32[]{:S(2)}) async-start(), calls=%async_computation.18 | async-start | bytes 11624448 | tf_op jit(solution)/shard_map/reduce_scatter | solution.py:331
  361.1 4670.1 %reduce-scatter.22.cloned.1.call-start = ((), (), s32[]{:S(2)}) async-start(), calls=%async_computation.19 | async-start | bytes 11624448 | tf_op jit(solution)/shard_map/reduce_scatter | solution.py:332
  375.3 4655.9 %copy-start.1 = (bf16[1024,1024]{1,0:T(8,128)(2,1)S(1)}, bf16[1024,1024]{1,0:T(8,128)(2,1)}, u32[]{:S(2)}) copy-start(bf16[1024,1024]{1,0:T(8,128)(2,1)} %param.30) | copy-start | bytes 6291460
  (63 other events, 185.7 us)
Sparse Core Ops, SparseCore 0:
  335.2 153.8 all-reduce.8
  492.1 639.3 reduce-scatter.11
  1134.4 634.1 reduce-scatter.13
  1771.5 637.8 reduce-scatter.15
  2412.2 637.9 reduce-scatter.9
  3053.1 657.3 reduce-scatter.17
  3713.6 657.3 reduce-scatter.19
  4374.1 657.0 reduce-scatter.21
where the time goes:
time: 5040 us
  waiting for transfers between devices  4630 us (92%)
  matrix products  145 us (3%)
  local copies, waits for them, and re-layouts  75.2 us (1%)
  blocking collectives  65.5 us (1%)
  other arithmetic  63.2 us (1%)
    reduce_scatter x1, waiting for transfers between devices, body(): lax.psum_scatter(grad_wup, ('seq', 'head'), scatter_dimension=0, tiled=True)  661 us
    reduce_scatter x1, waiting for transfers between devices, body(): lax.psum_scatter(grad_wgate, ('seq', 'head'), scatter_dimension=0, tiled=...  660 us
    reduce_scatter x1, waiting for transfers between devices, body(): lax.psum_scatter(grad_down, ('seq', 'head'), scatter_dimension=1, tiled=T...  660 us
    reduce_scatter x1, waiting for transfers between devices, body(): lax.psum_scatter(grad_wout, ('seq', 'head'), scatter_dimension=0, tiled=T...  641 us
    reduce_scatter x1, waiting for transfers between devices, body(): lax.psum_scatter(grad_wq, ('seq', 'head'), scatter_dimension=0, tiled=True)  641 us
    reduce_scatter x1, waiting for transfers between devices, body(): lax.psum_scatter(grad_wqr, ('seq', 'head'), scatter_dimension=0, tiled=True)  640 us
    reduce_scatter x1, waiting for transfers between devices, body(): lax.psum_scatter(grad_wlat, ('seq', 'head'), scatter_dimension=0, tiled=T...  637 us
  transfers between devices with their start and end apart: 14, of which 13 were waited for; matrix products, arithmetic and copies ran while one was open for 2% of the time, Pallas kernels for 0%

commit v1 on v0

--- a/solution.py
+++ b/solution.py
@@ -4,6 +4,8 @@
 import jax.numpy as jnp
 import numpy as np
 from jax import lax
+from jax.experimental import pallas as pl
+from jax.experimental.pallas import tpu as pltpu
 from jax.sharding import PartitionSpec as P
 
 HEADS = 16
@@ -62,6 +64,228 @@
     )
     grad_gain = jnp.sum(upstream * values * inverse, 0)
     return (grad_values, grad_gain)
+
+
+MESH = pl.DeviceIdType.MESH
+W = 256
+RING = 4
+ORDERS = (("y", "z", "x"), ("z", "x", "y"), ("x", "y", "z"))
+FIRST, LATER = 11, 4
+JOBS = FIRST + LATER
+
+
+def place():
+    s, h = lax.axis_index("seq"), lax.axis_index("head")
+    return {"y": s // 2, "core": s % 2, "z": h // 4, "x": h % 4}
+
+
+def device(at):
+    return (at["y"] * 2 + at["core"], at["z"] * 4 + at["x"])
+
+
+def beside(at, axis, step):
+    return device({**at, axis: (at[axis] + step) % 4})
+
+
+def other_core(at):
+    return device({**at, "core": 1 - at["core"]})
+
+
+def chosen_rows(order, core):
+    row = lax.broadcasted_iota(jnp.int32, (512, 1024), 0)
+    part = {"core": core}
+    for shift, axis in zip((7, 5, 3), order):
+        part[axis] = (row >> shift) & 3
+    column = (part["y"] << 8) + (core << 7) + (part["z"] << 5) + (part["x"] << 3) + (row & 7)
+    return (lax.broadcasted_iota(jnp.int32, (512, 1024), 1) == column).astype(jnp.bfloat16)
+
+
+def sum_kernel(*refs):
+    lefts, rights = refs[:6], refs[6:13]
+    (outs, at_own, at_send, at, g, d, s1, s2, sa, sb, sc, sd, se, sf, ra, rb, rc, rd, re, rf,
+     send_sem, recv_sem, at_sem, g_send, g_recv, g_local) = refs[13:]
+    me = place()
+    barrier = pltpu.get_barrier_semaphore()
+    peers = [other_core(me)] + [beside(me, a, s) for a in "xyz" for s in (1, -1)]
+    for peer in peers:
+        pl.semaphore_signal(barrier, inc=1, device_id=peer, device_id_type=MESH)
+    pl.semaphore_wait(barrier, len(peers))
+
+    def remote(src, dst, send, recv, to):
+        return pltpu.make_async_remote_copy(
+            src_ref=src, dst_ref=dst, send_sem=send, recv_sem=recv, device_id=to, device_id_type=MESH
+        )
+
+    twin = other_core(me)
+    sources = (((rights[0], 11), (rights[1], 4)), ((rights[2], 11), (rights[3], 4)), ((rights[4], 11), (rights[5], 2), (rights[6], 2)))
+    for order in range(3):
+        job = 0
+        for ref, count in sources[order]:
+            for c in range(count):
+                piece = ref.at[:, c * W : (c + 1) * W]
+                remote(piece, g.at[order, job, 128:256], g_send.at[order, job], g_recv.at[order, job], twin).start()
+                pltpu.make_async_copy(piece, g.at[order, job, 0:128], g_local.at[order, job]).start()
+                job += 1
+
+    def from_twin(order, job):
+        ref = g.at[order, job, 0:128]
+        return remote(ref, g.at[order, job, 128:256], g_send.at[order, job], g_recv.at[order, job], twin)
+
+    def from_here(order, job):
+        ref = g.at[order, job, 0:128]
+        return pltpu.make_async_copy(ref, ref, g_local.at[order, job])
+
+    for order in range(3):
+        for which in range(2):
+            left = lefts[order * 2 + which][...]
+            for mine in (0, 1):
+                core = me["core"] if mine else 1 - me["core"]
+                picked = lax.dot_general(chosen_rows(ORDERS[order], core), left, (((1,), (1,)), ((), ())), preferred_element_type=jnp.float32).astype(jnp.bfloat16)
+                if mine:
+                    at[order, which, :, 0:128] = picked
+                else:
+                    at_send[order, which] = picked
+                    remote(at_send.at[order, which], at.at[order, which, :, 128:256], at_sem.at[0, order, which], at_sem.at[1, order, which], twin).start()
+    for order in range(3):
+        for which in range(2):
+            remote(at_send.at[order, which], at.at[order, which, :, 128:256], at_sem.at[0, order, which], at_sem.at[1, order, which], twin).wait()
+
+    sends = (sa, sb, sc, sd, se, sf)
+    recvs = (ra, rb, rc, rd, re, rf)
+
+    def message(order, phase, way, job):
+        axis = ORDERS[order][phase // 2]
+        slot = job % RING
+        return remote(
+            sends[phase].at[order, slot, way],
+            recvs[phase].at[order, job, way],
+            send_sem.at[order, phase, way, slot],
+            recv_sem.at[order, phase, way, job],
+            beside(me, axis, 1 if way == 0 else -1),
+        )
+
+    def free(order, phase, job):
+        @pl.when(job >= RING)
+        def _():
+            for way in (0, 1):
+                message(order, phase, way, job - RING).wait_send()
+
+    def first_half(order, stage, job, block):
+        phase = stage * 2
+        free(order, phase, job)
+        for way in (0, 1):
+            ref = sends[phase].at[order, job % RING, way]
+            ref[...] = block[:, way * (W // 2) : (way + 1) * (W // 2)].astype(ref.dtype)
+            message(order, phase, way, job).start()
+
+    def second_half(order, stage, job, block_of):
+        phase = stage * 2 + 1
+        free(order, phase, job)
+        for way in (0, 1):
+            message(order, phase - 1, way, job).wait_recv()
+            ref = sends[phase].at[order, job % RING, way]
+            block = block_of(1 if way == 0 else -1)
+            here = slice(way * (W // 2), (way + 1) * (W // 2))
+            there = slice((1 - way) * (W // 2), (2 - way) * (W // 2))
+            ref[:, here] = (block[:, here] + recvs[phase - 1][order, job, way].astype(jnp.float32)).astype(ref.dtype)
+            ref[:, there] = block[:, there].astype(ref.dtype)
+            message(order, phase, way, job).start()
+
+    def total(order, stage, job, block):
+        phase = stage * 2 + 1
+        for way in (0, 1):
+            message(order, phase, way, job).wait_recv()
+            block = block + recvs[phase][order, job, way].astype(jnp.float32)
+        return block
+
+    def block_of(order, stage, job):
+        axis = ORDERS[order][stage]
+        slot = job % RING
+
+        def get(step):
+            index = (me[axis] + step) % 4
+            if stage == 0:
+                return d[order, slot, pl.ds(pl.multiple_of(index * 128, 128), 128), :]
+            if stage == 1:
+                return s1[order, slot, pl.ds(pl.multiple_of(index * 32, 32), 32), :]
+            return s2[order, slot, pl.ds(pl.multiple_of(index * 8, 8), 8), :]
+
+        return get
+
+    def step0(order, job):
+        from_twin(order, job).wait_recv()
+        from_here(order, job).wait()
+        which = jnp.where(job >= FIRST, 1, 0)
+        d[order, job % RING] = jnp.dot(at[order, which], g[order, job], preferred_element_type=jnp.float32)
+        first_half(order, 0, job, block_of(order, 0, job)(2))
+
+    def step1(order, job):
+        second_half(order, 0, job, block_of(order, 0, job))
+
+    def step2(order, job):
+        s1[order, job % RING] = total(order, 0, job, block_of(order, 0, job)(0))
+        first_half(order, 1, job, block_of(order, 1, job)(2))
+
+    def step3(order, job):
+        second_half(order, 1, job, block_of(order, 1, job))
+
+    def step4(order, job):
+        s2[order, job % RING] = total(order, 1, job, block_of(order, 1, job)(0))
+        first_half(order, 2, job, block_of(order, 2, job)(2))
+
+    def step5(order, job):
+        second_half(order, 2, job, block_of(order, 2, job))
+
+    def step6(order, job):
+        outs[order, :, pl.ds(pl.multiple_of(job * W, W), W)] = total(order, 2, job, block_of(order, 2, job)(0))
+
+    steps = (step0, step1, step2, step3, step4, step5, step6)
+
+    @pl.loop(0, JOBS + 6)
+    def _(t):
+        for k in reversed(range(7)):
+            job = t - k
+
+            @pl.when((job >= 0) & (job < JOBS))
+            def _():
+                for order in range(3):
+                    steps[k](order, job)
+
+    for order in range(3):
+        for phase in range(6):
+            for way in (0, 1):
+                for job in range(JOBS - RING, JOBS):
+                    message(order, phase, way, job).wait_send()
+
+        @pl.loop(0, JOBS)
+        def _(job):
+            from_twin(order, job).wait_send()
+
+
+def sum_gradients(lefts, rights):
+    bf, f32 = jnp.bfloat16, jnp.float32
+    vm = lambda shape, kind=bf: pltpu.VMEM(shape, kind)
+    dma = pltpu.SemaphoreType.DMA
+    R, J = RING, JOBS
+    return pl.pallas_call(
+        sum_kernel,
+        out_shape=jax.ShapeDtypeStruct((3, 8, JOBS * W), f32),
+        in_specs=[pl.BlockSpec(memory_space=pltpu.VMEM)] * 13,
+        out_specs=pl.BlockSpec(memory_space=pltpu.VMEM),
+        scratch_shapes=[
+            vm((8, 128)), vm((3, 2, 512, 128)), vm((3, 2, 512, 256)), vm((3, J, 256, W)),
+            vm((3, R, 512, W), f32), vm((3, R, 128, W), f32), vm((3, R, 32, W), f32),
+            vm((3, R, 2, 128, W // 2)), vm((3, R, 2, 128, W)),
+            vm((3, R, 2, 32, W // 2)), vm((3, R, 2, 32, W)),
+            vm((3, R, 2, 8, W // 2), f32), vm((3, R, 2, 8, W), f32),
+            vm((3, J, 2, 128, W // 2)), vm((3, J, 2, 128, W)),
+            vm((3, J, 2, 32, W // 2)), vm((3, J, 2, 32, W)),
+            vm((3, J, 2, 8, W // 2), f32), vm((3, J, 2, 8, W), f32),
+            dma((3, 6, 2, R)), dma((3, 6, 2, J)), dma((2, 3, 2)), dma((3, J)), dma((3, J)), dma((3, J)),
+        ],
+        compiler_params=pltpu.CompilerParams(collective_id=0, has_side_effects=True, vmem_limit_bytes=60 * 2**20),
+        name="sum_gradients",
+    )(*lefts, *rights)
 
 
 def body(
@@ -196,17 +420,13 @@
     output = (middle + jnp.dot(activated, w_down, preferred_element_type=jnp.float32)).astype(
         jnp.bfloat16
     )
-    grad_down = across(activated, cotangent)
     grad_act = against(cotangent, w_down)
     grad_gate = (grad_act * upward * sigma * (1.0 + gate * (1.0 - sigma))).astype(jnp.bfloat16)
     grad_upward = (grad_act * swish).astype(jnp.bfloat16)
-    grad_wgate = across(normed_two, grad_gate)
-    grad_wup = across(normed_two, grad_upward)
     grad_two = against(grad_gate, w_gate) + against(grad_upward, w_up)
     grad_mid_norm, grad_gain_two = norm_back(middle, inverse_two, gain_two, grad_two)
     grad_middle = cotangent.astype(jnp.float32) + grad_mid_norm
     grad_branch = grad_middle.astype(jnp.bfloat16)
-    grad_wout = across(attended, grad_branch)
     grad_attended = against(grad_branch, w_out).astype(jnp.bfloat16)
     head_grad = lax.all_to_all(
         grad_attended.reshape(local_rows, head_devs, query_width),
@@ -305,9 +525,6 @@
         .reshape(local_rows, HEADS * ROPE)
     )
     grad_kpre = rotate(grad_kturn, cosine, -sine).astype(jnp.bfloat16)
-    grad_wq = across(normed_one, grad_query_all)
-    grad_wqr = across(normed_one, grad_qrope)
-    grad_wlat = across(normed_one, grad_latent)
     grad_wkr = across(normed_one, grad_kpre)
     grad_one = (
         against(grad_query_all, w_query)
@@ -317,19 +534,23 @@
     )
     grad_in_norm, grad_gain_one = norm_back(inputs32, inverse_one, gain_one, grad_one)
     grad_input = grad_middle + grad_in_norm
+    parts = sum_gradients(
+        (normed_two, normed_one, normed_two, attended, cotangent, normed_one),
+        (grad_gate, grad_query_all, grad_upward, grad_branch, activated, grad_qrope, grad_latent),
+    )
     summed = (
         lax.psum_scatter(grad_gain_one, ("seq", "head"), scatter_dimension=0, tiled=True),
-        lax.psum_scatter(grad_wq, ("seq", "head"), scatter_dimension=0, tiled=True),
-        lax.psum_scatter(grad_wqr, ("seq", "head"), scatter_dimension=0, tiled=True),
-        lax.psum_scatter(grad_wlat, ("seq", "head"), scatter_dimension=0, tiled=True),
+        parts[0, :, 2816:],
+        parts[2, :, 2816:3328],
+        parts[2, :, 3328:],
         lax.psum_scatter(grad_wkr, ("seq", "head"), scatter_dimension=0, tiled=True),
         lax.psum_scatter(grad_kup, ("seq", "head"), scatter_dimension=2, tiled=True),
         lax.psum_scatter(grad_vup, ("seq", "head"), scatter_dimension=2, tiled=True),
-        lax.psum_scatter(grad_wout, ("seq", "head"), scatter_dimension=0, tiled=True),
+        parts[1, :, 2816:],
         lax.psum_scatter(grad_gain_two, ("seq", "head"), scatter_dimension=0, tiled=True),
-        lax.psum_scatter(grad_wgate, ("seq", "head"), scatter_dimension=0, tiled=True),
-        lax.psum_scatter(grad_wup, ("seq", "head"), scatter_dimension=0, tiled=True),
-        lax.psum_scatter(grad_down, ("seq", "head"), scatter_dimension=1, tiled=True),
+        parts[0, :, :2816],
+        parts[1, :, :2816],
+        parts[2, :, :2816].T,
     )
     return (
         output,

time: 5040 us -> 692 us (0.14)
  waiting for transfers between devices: 4630 us -> 182 us
  Pallas kernels: 0 us -> 108 us
    reduce_scatter x7 -> x0, waiting for transfers between devices: 4540 us -> none  [the longest x1 661 us: body(): lax.psum_scatter(grad_wup, ('seq', 'head'), scatter_dimension=0, tiled=True)]
    pallas_call x0 -> x1, Pallas kernels: none -> 108 us  [sum_gradients(): pl.pallas_call(sum_kernel, out_shape=jax.ShapeDtypeStruct((3, 8, JOBS * W...]
    unnamed x9 -> x2, waiting for transfers between devices: 43.4 us -> 146 us
  transfers between devices with their start and end apart: 14 -> 7, of which waited for: 13 -> 6; matrix products, arithmetic and copies ran while one was open for 2% -> 6% of each run, Pallas kernels for 0% -> 0%
where the time goes in v1:
time: 692 us; the launch traced here: 684 us
  waiting for transfers between devices  182 us (26%)
  matrix products  118 us (17%)
  Pallas kernels  108 us (16%)
  local copies, waits for them, and re-layouts  84.7 us (12%)
  other arithmetic  66.3 us (10%)
  blocking collectives  62.4 us (9%)
  starting transfers between devices  31.4 us (5%)
  loops' own time  16.1 us (2%)
  between operations  15.9 us (2%)
    unnamed x2, waiting for transfers between devices  146 us
    pallas_call x1, Pallas kernels, sum_gradients(): pl.pallas_call(sum_kernel, out_shape=jax.ShapeDtypeStruct((3, 8, JOBS * W...  108 us
    unnamed x1, blocking collectives  62.4 us
    unnamed x126, local copies, waits for them, and re-layouts  36.6 us
    dot_general x8, matrix products, scores(): jnp.einsum('bhr,kr->hbk', block_rope, group_key_rope, preferred_element_t...  17 us
    dot_general x10, matrix products, against(): lax.dot_general(left, right, (((1,), (1,)), ((), ())), preferred_element_...  16.4 us
    all_to_all x1, waiting for transfers between devices, body(): lax.all_to_all(latent_send, 'head', split_axis=1, concat_axis=0, tiled=True)  16 us
  transfers between devices with their start and end apart: 7, of which 6 were waited for; matrix products, arithmetic and copies ran while one was open for 6% of the time, Pallas kernels for 0%

profile of v1, /device:TPU:0, one launch (start us, length us, event | category | flops | bytes accessed | tf_op | source)
XLA Modules:
  0.0 684.4 jit_solution(1759550354353816306)
XLA Ops:
  21.4 8.0 %all-to-all-start = ((bf16[128,16,96]{0,2,1:T(8,128)(2,1)}), bf16[128,16,96]{0,2,1:T(8,128)(2,1)}, u32[]{:S(2)}, u32[]{:S(2)}) async-start(bf16[128,16,96]{0,2,1:T(8,128)(2,1)} %pad_maximum_fusion.2), calls=%async_computation | async-start | bytes 786432 | tf_op jit(solution)/shard_map/all_to_all | solution.py:355
  34.5 5.0 all-to-all-done
  39.6 4.0 all-to-all-start.1
  45.5 16.0 %all-to-all-done.1 = bf16[128,16,288]{0,2,1:T(8,128)(2,1)S(1)} async-done(((bf16[128,16,288]{0,2,1:T(8,128)(2,1)}), bf16[128,16,288]{0,2,1:T(8,128)(2,1)S(1)}, u32[]{:S(2)}, u32[]{:S(2)}) %all-to-all-start.1) | async-done | bytes 1179680 | tf_op jit(solution)/shard_map/all_to_all | solution.py:356
  67.1 45.6 %while.35 = (s32[]{:T(128)}, bf16[4,512,1,64]{1,3,2,0:T(8,128)(2,1)S(1)}, f32[4,1,512]{2,1,0:T(1,128)S(1)}, s32[4]{0:T(128)S(1)}, s32[]{:T(128)}, /*index=5*/bf1...) while((s32[]{:T(128)}, ...), condition=%wide.region_4.5_spmd.clone.clone, body=%wide.region_1.4_spmd.clone.clone.sunk | while | flops 348163072 | bytes 22213844 | solution.py:403
  116.8 12.6 %reduce.3 = bf16[2048,64]{1,0:T(8,128)(2,1)S(1)} reduce(bf16[2048,1,64]{2,1,0:T(2,128)(2,1)} %reshape.608, bf16[]{:T(256)} %broadcast.458), dimensions={1}, to_apply=%reshape.608.reduce_sub_computation | reduce | bytes 524290 | tf_op jit(solution)/shard_map/reshape | solution.py:405
  130.4 4.7 all-to-all-start.2
  135.2 8.6 %all-to-all-done.2 = bf16[16,2,4096]{2,1,0:T(2,128)(2,1)} async-done(((bf16[16,2,4096]{2,1,0:T(2,128)(2,1)}), bf16[16,2,4096]{2,1,0:T(2,128)(2,1)}, u32[]{:S(2)}, u32[]{:S(2)}) %all-to-all-start.2) | async-done | bytes 262176 | tf_op jit(solution)/shard_map/all_to_all | solution.py:404
  147.2 3.4 copy.92
  156.1 3.7 fusion.139
  174.4 3.7 all-to-all-start.3
  178.1 4.6 fusion.81
  182.6 4.1 all-to-all-done.3
  188.2 86.6 %while.36 = (s32[]{:T(128)}, f32[2048,1,64]{0,2,1:T(8,128)}, f32[2048,1,64]{0,2,1:T(8,128)S(1)}, f32[2048,32]{0,1:T(8,128)}, bf16[4,512,1,64]{1,3,2,0:T(8,128)(2...) while((s32[]{:T(128)}, f32[2048,1,64]{0,2,1:T(8,128)}, ...), condition=%wide.region_9.10_spmd.clone.clone.clone, body=%wide.region_7.9_spmd.clone.clone.clone.sunk | while | flops 887000064 | bytes 67423592 | solution.py:485
  282.1 3.6 all-to-all-start.4
  289.9 3.5 reduce.4
  295.9 5.2 reshape.616
  303.2 7.2 %all-to-all-start.5 = ((bf16[16,2,18432]{2,1,0:T(2,128)(2,1)}), bf16[16,2,18432]{2,1,0:T(2,128)(2,1)S(1)}, u32[]{:S(2)}, u32[]{:S(2)}) async-start(bf16[16,2,18432]{2,1,0:T(2,128)(2,1)} %reshape.616), calls=%async_computation.5 | async-start | bytes 2359296 | tf_op jit(solution)/shard_map/all_to_all | solution.py:508
  325.8 7.1 %reshape.617 = bf16[2048,1,288]{2,1,0:T(2,128)(2,1)} reshape(bf16[16,2,18432]{2,1,0:T(2,128)(2,1)S(1)} %all-to-all-done.5) | data formatting | bytes 2359296
  332.9 6.8 convert_bitcast_fusion
  339.7 5.7 copy.103
  348.8 107.9 %sum_gradients.1 = f32[3,8,3840]{2,1,0:T(8,128)} custom-call(bf16[128,1024]{1,0:T(8,128)(2,1)} %copy-done.7, bf16[128,1024]{1,0:T(8,128)(2,1)} %copy-done.4, bf16[128,1024]{1,0:T(8,128)(2,1)} %copy-done.7, bf16[128,1024]{1,0:T(8,128)(2,1)} %copy.107.refs_3_, bf16[128,1024]{1,0:T(8,128)(2,1)} %refs_4_.1, bf16[128,1024]{1,0:T(8,128)(2,1)} %copy-done.4, ...), custom_call_target="tpu_custom_call" | custom-call | tf_op jit(solution)/shard_map/sum_gradients/pallas_call | solution.py:270
  462.3 62.4 %all-reduce.5 = (f32[1024]{0:T(1024)S(1)}, f32[1024]{0:T(1024)S(1)}) all-reduce(f32[1024]{0:T(1024)S(1)} %get-tuple-element.405, f32[1024]{0:T(1024)S(1)} %copy-done.39), channel_id=2, replica_groups=mesh['seq'=8,'head'=16] {'seq','head'}, use_global_device_ids=true, to_apply=%region_14.15.clone | all-reduce | flops 2048 | bytes 16384
  528.6 146.0 %all-reduce.9.cloned.1.call-done = (f32[1024,32]{1,0:T(8,128)}, f32[2,256,512]{1,2,0:T(8,128)}, f32[2,256,512]{1,2,0:T(8,128)}) async-done(((f32[1024,32]{1,0:T(8,128)}, f32[2,256,512]{1,2,0:T(8,128)}, f32[2,256,512]{1,2,0:T(8,128)}), (f32[1024,32]{1,0:T(8,128)}, f32[2,256,512]{1,2,0:T(8,128)}, f32[2,256,512]{1,2,0:T(8,128)})) %all-reduce.9.cloned.1.call-update) | async-done | bytes 2228240
  (342 shorter events, 218.7 us)
Async XLA Ops:
  7.2 147.0 %copy-start = (bf16[1024,1024]{1,0:T(8,128)(2,1)S(1)}, bf16[1024,1024]{1,0:T(8,128)(2,1)}, u32[]{:S(2)}) copy-start(bf16[1024,1024]{1,0:T(8,128)(2,1)} %param.30) | copy-start | bytes 6291460
  11.6 17.8 %copy-start.4 = (bf16[128,1024]{1,0:T(8,128)(2,1)}, bf16[128,1024]{1,0:T(8,128)(2,1)S(1)}, u32[]{:S(2)}) copy-start(bf16[128,1024]{1,0:T(8,128)(2,1)S(1)} %fusion.86.refs_1_.refs_5_) | copy-start | bytes 786436
  21.4 18.2 %all-to-all-start = ((bf16[128,16,96]{0,2,1:T(8,128)(2,1)}), bf16[128,16,96]{0,2,1:T(8,128)(2,1)}, u32[]{:S(2)}, u32[]{:S(2)}) async-start(bf16[128,16,96]{0,2,1:T(8,128)(2,1)} %pad_maximum_fusion.2), calls=%async_computation | async-start | bytes 786432 | tf_op jit(solution)/shard_map/all_to_all | solution.py:355
  39.6 22.0 %all-to-all-start.1 = ((bf16[128,16,288]{0,2,1:T(8,128)(2,1)}), bf16[128,16,288]{0,2,1:T(8,128)(2,1)S(1)}, u32[]{:S(2)}, u32[]{:S(2)}) async-start(bf16[128,16,288]{0,2,1:T(8,128)(2,1)} %copy.87), calls=%async_computation.1 | async-start | bytes 2359296 | tf_op jit(solution)/shard_map/all_to_all | solution.py:356
  113.4 17.0 %copy-start.49 = (s32[4]{0:T(128)}, s32[4]{0:T(128)S(1)}, u32[]{:S(2)}) copy-start(s32[4]{0:T(128)S(1)} %get-tuple-element.782) | copy-start | bytes 52
  114.6 20.6 %copy-start.46 = (bf16[1024]{0:T(1024)(128)(2,1)S(1)}, bf16[1024]{0:T(1024)(128)(2,1)}, u32[]{:S(2)}) copy-start(bf16[1024]{0:T(1024)(128)(2,1)} %param.31) | copy-start | bytes 6148
  130.4 13.4 %all-to-all-start.2 = ((bf16[16,2,4096]{2,1,0:T(2,128)(2,1)}), bf16[16,2,4096]{2,1,0:T(2,128)(2,1)}, u32[]{:S(2)}, u32[]{:S(2)}) async-start(bf16[16,2,4096]{2,1,0:T(2,128)(2,1)} %reshape.614), calls=%async_computation.2 | async-start | bytes 524288 | tf_op jit(solution)/shard_map/all_to_all | solution.py:404
  174.4 12.4 %all-to-all-start.3 = ((bf16[128,16,64]{0,2,1:T(8,128)(2,1)}), bf16[128,16,64]{0,2,1:T(8,128)(2,1)S(1)}, u32[]{:S(2)}, u32[]{:S(2)}) async-start(bf16[128,16,64]{0,2,1:T(8,128)(2,1)} %bitcast.16), calls=%async_computation.3 | async-start | bytes 524288 | tf_op jit(solution)/shard_map/all_to_all | solution.py:431
  282.1 21.1 %all-to-all-start.4 = ((bf16[16,2,6144]{2,1,0:T(2,128)(2,1)}), bf16[16,2,6144]{2,1,0:T(2,128)(2,1)S(1)}, u32[]{:S(2)}, u32[]{:S(2)}) async-start(bf16[16,2,6144]{2,1,0:T(2,128)(2,1)} %reshape.618), calls=%async_computation.4 | async-start | bytes 786432 | tf_op jit(solution)/shard_map/all_to_all | solution.py:495
  303.2 22.6 %all-to-all-start.5 = ((bf16[16,2,18432]{2,1,0:T(2,128)(2,1)}), bf16[16,2,18432]{2,1,0:T(2,128)(2,1)S(1)}, u32[]{:S(2)}, u32[]{:S(2)}) async-start(bf16[16,2,18432]{2,1,0:T(2,128)(2,1)} %reshape.616), calls=%async_computation.5 | async-start | bytes 2359296 | tf_op jit(solution)/shard_map/all_to_all | solution.py:508
  310.4 364.3 %all-reduce.9.cloned.1.call-start = ((), (), s32[]{:S(2)}) async-start(), calls=%async_computation.6 | async-start | bytes 5242880
  348.7 110.8 %copy-start.43 = (f32[16]{0:T(128)S(1)}, f32[16]{0:T(128)}, u32[]{:S(2)}) copy-start(f32[16]{0:T(128)} %copy-done.42) | copy-start | bytes 196
  348.7 110.8 %copy-start.45 = (f32[128]{0:T(128)S(1)}, f32[128]{0:T(128)}, u32[]{:S(2)}) copy-start(f32[128]{0:T(128)} %copy-done.44) | copy-start | bytes 1540
  348.7 110.9 %copy-start.32 = (bf16[1024,32]{0,1:T(8,128)(2,1)S(1)}, bf16[1024,32]{0,1:T(8,128)(2,1)}, u32[]{:S(2)}) copy-start(bf16[1024,32]{0,1:T(8,128)(2,1)} %param.27) | copy-start | bytes 196612
  348.7 111.2 %copy-start.5 = (bf16[128,1024]{1,0:T(8,128)(2,1)S(1)}, bf16[128,1024]{1,0:T(8,128)(2,1)}, u32[]{:S(2)}) copy-start(bf16[128,1024]{1,0:T(8,128)(2,1)} %copy-done.4) | copy-start | bytes 786436
  348.7 112.2 %copy-start.15 = (bf16[128,1024]{1,0:T(8,128)(2,1)S(1)}, bf16[128,1024]{1,0:T(8,128)(2,1)}, u32[]{:S(2)}) copy-start(bf16[128,1024]{1,0:T(8,128)(2,1)} %param.21) | copy-start | bytes 786436
  348.7 112.2 %copy-start.18 = (bf16[1024,512]{1,0:T(8,128)(2,1)S(1)}, bf16[1024,512]{1,0:T(8,128)(2,1)}, u32[]{:S(2)}) copy-start(bf16[1024,512]{1,0:T(8,128)(2,1)} %param.26) | copy-start | bytes 3145732
  348.8 112.2 %copy-start.26 = (bf16[16,8,2,256]{3,1,2,0:T(8,128)(2,1)S(1)}, bf16[16,8,2,256]{3,1,2,0:T(8,128)(2,1)}, u32[]{:S(2)}) copy-start(bf16[16,8,2,256]{3,1,2,0:T(8,128)(2,1)} %copy.128) | copy-start | bytes 393220
  348.8 112.2 %copy-start.37 = (f32[1024]{0:T(1024)S(1)}, f32[1024]{0:T(1024)}, u32[]{:S(2)}) copy-start(f32[1024]{0:T(1024)} %copy-done.36) | copy-start | bytes 12292
  348.8 112.2 %copy-start.41 = (f32[128]{0:T(128)S(1)}, f32[128]{0:T(128)}, u32[]{:S(2)}) copy-start(f32[128]{0:T(128)} %copy-done.40) | copy-start | bytes 1540
  461.0 64.9 %copy-start.24 = (f32[128,1024]{1,0:T(8,128)S(1)}, f32[128,1024]{1,0:T(8,128)}, u32[]{:S(2)}) copy-start(f32[128,1024]{1,0:T(8,128)} %get-tuple-element.463) | copy-start | bytes 1572868
  461.0 64.9 %copy-start.48 = (f32[128]{0:T(128)S(1)}, f32[128]{0:T(128)}, u32[]{:S(2)}) copy-start(f32[128]{0:T(128)} %get-tuple-element.491) | copy-start | bytes 1540
  462.3 63.6 %copy-start.25 = (f32[128,1024]{1,0:T(8,128)S(1)}, f32[128,1024]{1,0:T(8,128)}, u32[]{:S(2)}) copy-start(f32[128,1024]{1,0:T(8,128)} %get-tuple-element.498) | copy-start | bytes 1572868
  525.3 152.0 %copy-start.1 = (bf16[1024,1024]{1,0:T(8,128)(2,1)S(1)}, bf16[1024,1024]{1,0:T(8,128)(2,1)}, u32[]{:S(2)}) copy-start(bf16[1024,1024]{1,0:T(8,128)(2,1)} %param.30) | copy-start | bytes 6291460
  (50 other events, 212.9 us)
Sparse Core Ops, SparseCore 0:
  526.0 148.6 all-reduce.8

commit v2 on v0

v2 whole, which is shorter than its diff:
```python
import math
import types
import numpy as np
import jax
import jax.numpy as jnp
from jax import lax
from jax.experimental import pallas as pl
from jax.experimental.pallas import tpu as pltpu
from jax.sharding import PartitionSpec as P

MESH = pl.DeviceIdType.MESH
bf, f32 = jnp.bfloat16, jnp.float32
W = 256
EPS = 1e-6
SCALE = 1.0 / math.sqrt(96)
DEPTH = 4


def dot(a, b, ca=1, cb=0):
    return lax.dot_general(a, b, (((ca,), (cb,)), ((), ())), preferred_element_type=f32)


def place():
    s, h = lax.axis_index("seq"), lax.axis_index("head")
    return {"y": s // 2, "core": s % 2, "z": h // 4, "x": h % 4}


def device(at):
    return (at["y"] * 2 + at["core"], at["z"] * 4 + at["x"])


def remote(src, dst, send, recv, to):
    return pltpu.make_async_remote_copy(
        src_ref=src, dst_ref=dst, send_sem=send, recv_sem=recv, device_id=to, device_id_type=MESH
    )


def lanes(start, size):
    return pl.ds(pl.multiple_of(start, size), size)


def rows_of(block):
    return pl.ds(pl.multiple_of((block % 2) * 128, 128), 128)


def turn(u, cosine, sine):
    first, second = u[..., :16, :], u[..., 16:, :]
    return jnp.concatenate([first * cosine - second * sine, first * sine + second * cosine], -2)


def load_first(r, again=False):
    for i in range(2):
        pltpu.make_async_copy(r.wq.at[:, i * 512 : (i + 1) * 512], r.pool.at[i], r.first_sem.at[i]).start()
    pltpu.make_async_copy(r.wqr, r.pool.at[2], r.first_sem.at[2]).start()
    pltpu.make_async_copy(r.wl, r.pool.at[3], r.first_sem.at[3]).start()
    if not again:
        pltpu.make_async_copy(r.wo_hbm, r.wo, r.first_sem.at[4]).start()


def wait_first(r, i):
    ref = r.wo if i == 4 else r.pool.at[i]
    pltpu.make_async_copy(ref, ref, r.first_sem.at[i]).wait()


def chunk_copies(r, j):
    slot = j % DEPTH
    here = lanes(j * W, W)
    return (
        pltpu.make_async_copy(r.wg.at[:, here], r.pool.at[slot, :, 0:W], r.chunk_sem.at[slot, 0]),
        pltpu.make_async_copy(r.wu.at[:, here], r.pool.at[slot, :, W : 2 * W], r.chunk_sem.at[slot, 1]),
        pltpu.make_async_copy(r.wd.at[here, :], r.wdpool.at[slot], r.chunk_sem.at[slot, 2]),
    )


def project(r, seq, h):
    x = r.x[...].astype(f32)
    inverse = lax.rsqrt(jnp.mean(x * x, -1, keepdims=True) + EPS)
    n1 = (x * inverse * r.gain1[...].astype(f32)).astype(bf)
    r.n1[...] = n1
    bound = r.second[0]
    token = h * 128 + lax.broadcasted_iota(jnp.int32, (16, 128), 1)
    position = token - jnp.where(token >= bound, bound, 0)
    angle = position.astype(f32) * r.freq[...]
    cosine, sine = jnp.cos(angle), jnp.sin(angle)
    r.cos[...], r.sin[...] = cosine, sine
    wait_first(r, 3)
    lat = dot(n1, r.pool[3]).astype(bf)
    kr = turn(dot(r.wkr[...], n1, 1, 1), cosine, sine)
    flag = jnp.where(h == 15, 0.0, 1.0)
    flags = jnp.where(lax.broadcasted_iota(jnp.int32, (96, 128), 0) == 0, flag, 0.0)
    own = jnp.concatenate([kr, flags], 0).T.astype(bf)
    b = h // 2
    mine = r.lx.at[b, rows_of(h)]
    mine[:, 0:256] = lat[:, 0:256]
    mine[:, 256:384] = own
    mine[:, 384:640] = lat[:, 256:512]

    @pl.when(h % 2 == 0)
    def _():
        r.lx[b, 128:256] = jnp.zeros((128, 640), bf)

    for k in range(1, 16):
        @pl.when(h + k < 16)
        def _():
            remote(mine, mine, r.gather_send.at[k], r.gather_recv.at[h], (seq, h + k)).start()

    for i in range(2):
        wait_first(r, i)
        r.qt[i * 512 : (i + 1) * 512] = dot(n1, r.pool[i]).T.astype(bf)
    wait_first(r, 2)
    qr = (turn(dot(n1, r.pool[2]).T.reshape(16, 32, 128), cosine, sine) * SCALE).astype(bf)
    for j in range(DEPTH):
        for copy in chunk_copies(r, j):
            copy.start()
    late = (h * 128 + (lax.broadcasted_iota(jnp.int32, (96, 1024), 1) & 127)) >= bound
    bias = jnp.where(late & (lax.broadcasted_iota(jnp.int32, (96, 1024), 0) == 0), -1e30, 0.0).astype(bf)
    for g in range(2):
        kt = r.kup[g].T
        r.kt[g] = kt
        r.vt[g] = r.vup[g].T
        at, rope = (0, 256) if g == 0 else (128, 0)
        r.qxt[g, rope + 32 : rope + 128] = bias
        for e in range(8):
            head = g * 8 + e
            cols = slice(e * 128, (e + 1) * 128)
            r.qxt[g, rope : rope + 32, cols] = qr[head]
            r.qxt[g, at : at + 256, cols] = (
                dot(r.kt[g, e * 64 : (e + 1) * 64, :], r.qt[head * 64 : (head + 1) * 64], 0, 0) * SCALE
            ).astype(bf)


def gather_wait(r, seq, h, i):
    ref = r.lx.at[i // 2, rows_of(i)]

    @pl.when(i < h)
    def _():
        remote(ref, ref, r.gather_send.at[0], r.gather_recv.at[i], (seq, 0)).wait_recv()


def attend_step(r, seq, h, b, diag):
    gather_wait(r, seq, h, 2 * b)
    gather_wait(r, seq, h, 2 * b + 1)
    r.lxt[...] = r.lx[b].T
    if diag:
        bound = r.second[0]
        key = b * 256 + lax.broadcasted_iota(jnp.int32, (256, 128), 0)
        row = h * 128 + lax.broadcasted_iota(jnp.int32, (256, 128), 1)
        ok = (key <= row) & ((key >= bound) == (row >= bound))
        mask = jnp.where(ok, 0.0, 1.0)
        mask = jnp.concatenate([mask, mask], 1)
    for g in range(2):
        at = 0 if g == 0 else 384
        for c in range(4):
            cols = slice(c * 256, (c + 1) * 256)
            s = dot(r.lx[b, :, g * 256 : g * 256 + 384], r.qxt[g, :, cols])
            if diag:
                s = jnp.where(mask > 0.5, -1e30, s)
            top = jnp.max(s, 0, keepdims=True)
            if not diag:
                before = r.top[g : g + 1, cols]
                top = jnp.maximum(top, before)
            p = jnp.exp(s - top)
            total = jnp.sum(p, 0, keepdims=True)
            pb = p.astype(bf)
            r.p[b, g, :, cols] = pb
            o = dot(r.lxt[at : at + 256], pb)
            if not diag:
                fade = jnp.exp(before - top)
                total = total + r.total[g : g + 1, cols] * fade
                o = o + r.acc[g, 0:256, cols] * fade
            r.acc[g, 0:256, cols] = o
            r.total[g : g + 1, cols] = total
            r.top[g : g + 1, cols] = top
            r.tops[b, g : g + 1, cols] = top


def attend(r, seq, h):
    last = h // 2
    attend_step(r, seq, h, last, True)

    @pl.loop(0, last)
    def _(i):
        attend_step(r, seq, h, last - 1 - i, False)

    for g in range(2):
        back = 1.0 / r.total[g : g + 1]
        r.back[g : g + 1] = back
        r.ot[g] = (r.acc[g, 0:256] * back).astype(bf)
        for e in range(8):
            head = g * 8 + e
            r.attt[head * 64 : (head + 1) * 64] = dot(
                r.vt[g, e * 64 : (e + 1) * 64], r.ot[g, :, e * 128 : (e + 1) * 128]
            ).astype(bf)
    r.att[...] = r.attt[...].T


def feed(r, begin, each):
    wait_first(r, 4)
    r.mid[...] = r.x[...].astype(f32) + dot(r.att[...], r.wo[...])
    mid = r.mid[...]
    inverse = lax.rsqrt(jnp.mean(mid * mid, -1, keepdims=True) + EPS)
    gain = r.gain2[...].astype(f32)
    r.n2[...] = (mid * inverse * gain).astype(bf)
    r.grad_input[...] = mid
    r.g_acc[...] = jnp.zeros((128, 1024), f32)
    begin()

    @pl.loop(0, 11)
    def _(j):
        slot = j % DEPTH
        for copy in chunk_copies(r, j):
            copy.wait()
        n2, cot = r.n2[...], r.cot[...]
        gate = dot(n2, r.pool[slot, :, 0:W])
        up = dot(n2, r.pool[slot, :, W : 2 * W])
        grad = dot(cot, r.wdpool[slot], 1, 1)
        sigma = jax.nn.sigmoid(gate)
        swish = gate * sigma
        act = (swish * up).astype(bf)
        grad_gate = (grad * up * sigma * (1.0 + gate * (1.0 - sigma))).astype(bf)
        grad_up = (grad * swish).astype(bf)
        r.grad_input[...] += dot(act, r.wdpool[slot])
        r.g_acc[...] += dot(grad_gate, r.pool[slot, :, 0:W], 1, 1) + dot(grad_up, r.pool[slot, :, W : 2 * W], 1, 1)

        @pl.when(j + DEPTH < 11)
        def _():
            for copy in chunk_copies(r, j + DEPTH):
                copy.start()

        each(j, grad_gate, grad_up, act)

    r.output[...] = r.grad_input[...].astype(bf)
    up = r.g_acc[...]
    mid = r.mid[...]
    inverse = lax.rsqrt(jnp.mean(mid * mid, -1, keepdims=True) + EPS)
    r.gains[1:2] = jnp.sum(up * mid * inverse, 0, keepdims=True)
    scaled = up * gain
    grad_mid = r.cot[...].astype(f32) + inverse * scaled - mid * (inverse * inverse * inverse) * jnp.mean(mid * scaled, -1, keepdims=True)
    r.mid[...] = grad_mid
    r.gb[...] = grad_mid.astype(bf)
    r.ga[...] = dot(r.gb[...], r.wo[...], 1, 1).T.astype(bf)


RING = 4
ORDERS = (("y", "z", "x"), ("z", "x", "y"), ("x", "y", "z"))
EARLY = (12, 13, 13)
JOBS = 16
FEED, OUT, ONE = 0, 1, 2
PHASES = ("a", "b", "c", "d", "e", "f")


def beside(at, axis, step):
    return device({**at, axis: (at[axis] + step) % 4})


def other_core(at):
    return device({**at, "core": 1 - at["core"]})


def choose_rows(r, me, order, which):
    for mine in (True, False):
        core = me["core"] if mine else 1 - me["core"]
        parts = []
        for i in range(64):
            part = dict(zip(ORDERS[order], (i >> 4, (i >> 2) & 3, i & 3)))
            start = part["y"] * 256 + part["z"] * 32 + part["x"] * 8
            parts.append(r.nt[pl.ds(pl.multiple_of(core * 128 + start, 8), 8), :])
        picked = jnp.concatenate(parts, 0).astype(bf)
        if mine:
            r.at[order, which, :, 0:128] = picked
        else:
            r.at_send[order, which] = picked
    at_copy(r, me, order, which).start()


def at_copy(r, me, order, which):
    return remote(
        r.at_send.at[order, which], r.at.at[order, which, :, 128:256],
        r.at_sem.at[0, order, which], r.at_sem.at[1, order, which], other_core(me),
    )


def g_copy(r, me, order, job):
    return remote(
        r.g.at[order, job, 0:128], r.g.at[order, job, 128:256],
        r.g_send.at[order, job], r.g_recv.at[order, job], other_core(me),
    )


def give(r, me, order, job, value):
    r.g[order, job, 0:128] = value
    g_copy(r, me, order, job).start()


def dense_copy(r, me, which):
    return remote(
        r.dense_send.at[which], r.dense.at[which, :, 128:256],
        r.dense_sem.at[0, which], r.dense_sem.at[1, which], other_core(me),
    )


def give_heads(r, me, which, left, right):
    for mine in (True, False):
        core = me["core"] if mine else 1 - me["core"]
        for q in range(4):
            for g in range(2):
                e = q * 2 + core
                rows = lanes((g * 8 + e) * 64, 64)
                block = dot(left[rows, :], right[g, :, lanes(e * 128, 128)], 1, 1).astype(bf)
                if mine:
                    r.dense[which, q, g * 64 : g * 64 + 64] = block
                else:
                    r.dense_send[which, q, g * 64 : g * 64 + 64] = block
    dense_copy(r, me, which).start()


def message(r, me, order, phase, way, job):
    slot = job % RING
    kind = PHASES[phase]
    return remote(
        getattr(r, "s" + kind).at[order, slot, way],
        getattr(r, "r" + kind).at[order, slot, way],
        r.sum_send.at[order, phase, way, slot],
        r.sum_recv.at[order, phase, way, slot],
        beside(me, ORDERS[order][phase // 2], 1 if way == 0 else -1),
    )


def first_half(r, me, order, stage, job, block):
    phase = stage * 2

    @pl.when(job >= RING)
    def _():
        for way in (0, 1):
            message(r, me, order, phase, way, job - RING).wait_send()

    ref = getattr(r, "s" + PHASES[phase])
    for way in (0, 1):
        half = block[:, way * (W // 2) : (way + 1) * (W // 2)]
        ref[order, job % RING, way] = half.astype(ref.dtype)
        message(r, me, order, phase, way, job).start()


def second_half(r, me, order, stage, job, block_of):
    phase = stage * 2 + 1

    @pl.when(job >= RING)
    def _():
        for way in (0, 1):
            message(r, me, order, phase, way, job - RING).wait_send()

    ref, got = getattr(r, "s" + PHASES[phase]), getattr(r, "r" + PHASES[phase - 1])
    slot = job % RING
    for way in (0, 1):
        message(r, me, order, phase - 1, way, job).wait_recv()
        block = block_of(1 if way == 0 else -1)
        here = slice(way * (W // 2), (way + 1) * (W // 2))
        there = slice((1 - way) * (W // 2), (2 - way) * (W // 2))
        ref[order, slot, way, :, here] = (block[:, here] + got[order, slot, way].astype(f32)).astype(ref.dtype)
        ref[order, slot, way, :, there] = block[:, there].astype(ref.dtype)
        message(r, me, order, phase, way, job).start()


def total(r, me, order, stage, job, block):
    phase = stage * 2 + 1
    got = getattr(r, "r" + PHASES[phase])
    for way in (0, 1):
        message(r, me, order, phase, way, job).wait_recv()
        block = block + got[order, job % RING, way].astype(f32)
    return block


def block_of(r, me, order, stage, job):
    axis = ORDERS[order][stage]
    slot = job % RING

    def get(step):
        index = (me[axis] + step) % 4
        if stage == 0:
            return r.d[order, slot, lanes(index * 128, 128), :].astype(f32)
        if stage == 1:
            return r.s1[order, slot, lanes(index * 32, 32), :]
        return r.s2[order, slot, lanes(index * 8, 8), :]

    return get


def products(r, me, order, job, late):
    slot = job % RING

    def plain(which):
        g_copy(r, me, order, job).wait_recv()
        r.d[order, slot] = dot(r.at[order, which], r.g[order, job]).astype(bf)

    def thick(which):
        dense_copy(r, me, which).wait_recv()
        row = lax.broadcasted_iota(jnp.int32, (128, 256), 0)
        column = lax.broadcasted_iota(jnp.int32, (128, 256), 1) & 127
        if which < 2:
            row = ((row >> 2) & 1) * 64 + (row >> 3) * 4 + (row & 3)
        pick = (row == column).astype(bf)
        for q in range(4):
            r.d[order, slot, q * 128 : (q + 1) * 128] = dot(pick, r.dense[which, q]).astype(bf)

    if order == 0:
        if late:
            pl.when(job == 12)(lambda: thick(1))
            pl.when((job == 13) | (job == 14))(lambda: plain(ONE))
            pl.when(job == 15)(lambda: thick(2))
        else:
            pl.when(job < 11)(lambda: plain(FEED))
            pl.when(job == 11)(lambda: thick(0))
    elif late:
        plain(ONE)
    else:
        plain(jnp.where(job < 11, FEED, OUT))


def sum_step(r, me, order, k, job, late):
    get = block_of(r, me, order, min(k // 2, 2), job)
    if k == 0:
        products(r, me, order, job, late)
        first_half(r, me, order, 0, job, get(2))
    elif k % 2:
        second_half(r, me, order, k // 2, job, get)
    elif k == 2:
        r.s1[order, job % RING] = total(r, me, order, 0, job, block_of(r, me, order, 0, job)(0))
        first_half(r, me, order, 1, job, get(2))
    elif k == 4:
        r.s2[order, job % RING] = total(r, me, order, 1, job, block_of(r, me, order, 1, job)(0))
        first_half(r, me, order, 2, job, get(2))
    else:
        own = block_of(r, me, order, 2, job)(0)
        r.sums[order, :, lanes(job * W, W)] = total(r, me, order, 2, job, own)


def sum_slot(r, me, t, late=False):
    for k in reversed(range(7)):
        for order in range(3):
            base = EARLY[order] if late else 0
            end = JOBS if late else EARLY[order]
            job = base + t - 1 - k

            @pl.when((job >= base) & (job < end))
            def _():
                sum_step(r, me, order, k, job, late)


def sum_end(r, me):
    for order in range(3):
        for phase in range(6):
            for way in (0, 1):
                for job in range(JOBS - RING, JOBS):
                    message(r, me, order, phase, way, job).wait_send()
        for job in range(JOBS):
            if order or job < 11 or job in (13, 14):
                g_copy(r, me, order, job).wait_send()
        for which in (FEED, OUT, ONE):
            if order or which != OUT:
                at_copy(r, me, order, which).wait_send()
    for which in range(3):
        dense_copy(r, me, which).wait_send()


def wait_rows(r, me, which):
    for order in range(3):
        if order or which != OUT:
            at_copy(r, me, order, which).wait_recv()


def prepare_back(r):
    for g in range(2):
        r.qxn[g] = r.qxt[g].T
        for e in range(8):
            head = g * 8 + e
            cols = slice(e * 128, (e + 1) * 128)
            ga = r.ga[head * 64 : (head + 1) * 64]
            back = r.back[g : g + 1, cols]
            inner = jnp.sum(ga.astype(f32) * r.attt[head * 64 : (head + 1) * 64].astype(f32), 0, keepdims=True)
            r.inner[g : g + 1, cols] = inner * back
            r.dt[g, :, cols] = (dot(r.vt[g, e * 64 : (e + 1) * 64, :], ga, 0, 0) * back).astype(bf)
        r.dn[g] = r.dt[g].T
    r.acc[...] = jnp.zeros((2, 384, 1024), f32)


def latent_copy(r, seq, h, b, s):
    slot = b % 4
    return remote(
        r.wdpool.at[slot, s * 128 : s * 128 + 128, 0:640], r.lg.at[h],
        r.lg_send.at[slot, s], r.lg_recv.at[h], (seq, b * 2 + s),
    )


def back_step(r, seq, h, b):
    @pl.when(b >= 4)
    def _():
        for s in (0, 1):
            latent_copy(r, seq, h, b - 4, s).wait_send()

    slot = b % 4
    r.lxt[...] = r.lx[b].T
    rope = None
    for g in range(2):
        at = 0 if g == 0 else 384
        for c in range(4):
            cols = slice(c * 256, (c + 1) * 256)
            fade = jnp.exp(r.tops[b, g : g + 1, cols] - r.top[g : g + 1, cols])
            p = r.p[b, g, :, cols].astype(f32) * fade
            dp = dot(r.lx[b, :, at : at + 256], r.dt[g, :, cols])
            r.ds[:, cols] = (p * (dp - r.inner[g : g + 1, cols])).astype(bf)
            r.pf[:, cols] = p.astype(bf)
        ds = r.ds[...]
        gl = dot(ds, r.qxn[g])
        gp = dot(r.pf[...], r.dn[g])
        r.acc[g] += dot(r.lxt[g * 256 : g * 256 + 384], ds)
        if g == 0:
            left = gl[:, 0:256] + gp
            rope = gl[:, 256:384]
        else:
            rope = rope + gl[:, 0:128]
            right = gl[:, 128:384] + gp
    whole = jnp.concatenate([left, rope, right], 1)
    r.wdpool[slot, :, 0:640] = whole.astype(bf)
    for s in (0, 1):
        @pl.when(2 * b + s < h)
        def _():
            latent_copy(r, seq, h, b, s).start()

        @pl.when(2 * b + s == h)
        def _():
            r.own[...] = whole[s * 128 : s * 128 + 128]


def back_end(r, seq, h):
    last = h // 2
    for d in range(4):
        b = last - d
        for s in (0, 1):
            @pl.when((b >= 0) & (2 * b + s < h))
            def _():
                latent_copy(r, seq, h, b, s).wait_send()


def finish_queries(r, me):
    for g in range(2):
        at, rope = (0, 256) if g == 0 else (128, 0)
        r.ot[g] = (r.acc[g, at : at + 256] * SCALE).astype(bf)
        for e in range(8):
            head = g * 8 + e
            cols = slice(e * 128, (e + 1) * 128)
            r.attt[head * 64 : (head + 1) * 64] = dot(r.kt[g, e * 64 : (e + 1) * 64], r.ot[g, :, cols]).astype(bf)
            turned = (r.acc[g, rope : rope + 32, cols] * SCALE).astype(bf).astype(f32)
            r.nt[head * 32 : (head + 1) * 32] = turn(turned, r.cos[...], -r.sin[...])
    r.n2[...] = r.attt[...].T
    r.gb[:, 0:512] = r.nt[0:512].T.astype(bf)
    for c in range(3):
        give(r, me, 1, 13 + c, r.n2[:, c * 256 : (c + 1) * 256])
    give(r, me, 2, 13, r.n2[:, 768:1024])
    for c in range(2):
        give(r, me, 0, 13 + c, r.gb[:, c * 256 : (c + 1) * 256])
    give_heads(r, me, 1, r.qt, r.ot)


def finish_latent(r, me, seq, h):
    @pl.loop(0, 16)
    def _(j):
        @pl.when(j > h)
        def _():
            remote(r.lg.at[j], r.lg.at[j], r.lg_send.at[0, 0], r.lg_recv.at[j], (seq, 0)).wait_recv()
            r.own[...] += r.lg[j].astype(f32)

    r.gb[:, 512:768] = r.own[:, 0:256].astype(bf)
    r.gb[:, 768:1024] = r.own[:, 384:640].astype(bf)
    for c in range(2):
        give(r, me, 2, 14 + c, r.gb[:, 512 + c * 256 : 768 + c * 256])
    turned = r.own[:, 256:384].astype(bf).astype(f32).T[0:32]
    kr = turn(turned, r.cos[...], -r.sin[...])
    r.gkr[...] = jnp.concatenate([kr, jnp.zeros((96, 128), f32)], 0).T.astype(bf)


def finish_input(r):
    grad = dot(r.gkr[:, 0:32], r.wkr[...])
    for i in range(2):
        grad = grad + dot(r.n2[:, i * 512 : (i + 1) * 512], r.pool[i], 1, 1)
    grad = grad + dot(r.gb[:, 0:512], r.pool[2], 1, 1) + dot(r.gb[:, 512:1024], r.pool[3], 1, 1)
    x = r.x[...].astype(f32)
    inverse = lax.rsqrt(jnp.mean(x * x, -1, keepdims=True) + EPS)
    r.gains[0:1] = jnp.sum(grad * x * inverse, 0, keepdims=True)
    scaled = grad * r.gain1[...].astype(f32)
    r.grad_input[...] = r.mid[...] + inverse * scaled - x * (inverse * inverse * inverse) * jnp.mean(x * scaled, -1, keepdims=True)


def finish_rope(r, me):
    wide = jnp.concatenate([r.gkr[...], jnp.zeros((128, 128), bf)], 1)
    row = lax.broadcasted_iota(jnp.int32, (16, 256), 0)
    column = lax.broadcasted_iota(jnp.int32, (16, 256), 1)
    spread = ((row < 4) & (column == 32 + row // 2)).astype(bf)
    for mine in (True, False):
        core = me["core"] if mine else 1 - me["core"]
        for q in range(4):
            gains = r.gains[0:2, lanes(q * 256 + core * 128, 128)]
            high = gains.astype(bf).astype(f32)
            low = gains - high
            stack = jnp.concatenate([high[0:1], low[0:1], high[1:2], low[1:2], jnp.zeros((12, 128), f32)], 0).astype(bf)
            left = r.at[0, ONE, q * 128 : (q + 1) * 128, 0:128] if mine else r.at_send[0, ONE, q * 128 : (q + 1) * 128]
            block = (dot(left, wide) + dot(stack, spread, 0, 0)).astype(bf)
            if mine:
                r.dense[2, q, 0:128] = block
            else:
                r.dense_send[2, q] = block
    dense_copy(r, me, 2).start()


INPUTS = ("x", "cot", "second", "gain1", "gain2", "freq", "wkr", "kup", "vup", "wq", "wqr", "wl", "wo_hbm", "wg", "wu", "wd")


def scratch():
    vm = lambda *shape, kind=bf: pltpu.VMEM(shape, kind)
    dma = pltpu.SemaphoreType.DMA
    return dict(
        pool=vm(4, 1024, 512), wdpool=vm(4, 256, 1024), wo=vm(1024, 1024),
        first_sem=dma((5,)), chunk_sem=dma((4, 3)),
        n1=vm(128, 1024), n2=vm(128, 1024), gb=vm(128, 1024), ga=vm(1024, 128), att=vm(128, 1024), attt=vm(1024, 128),
        cos=vm(16, 128, kind=f32), sin=vm(16, 128, kind=f32),
        lx=vm(8, 256, 640), lxt=vm(640, 256), qt=vm(1024, 128), kt=vm(2, 512, 256), vt=vm(2, 512, 256),
        qxt=vm(2, 384, 1024), p=vm(8, 2, 256, 1024), acc=vm(2, 384, 1024, kind=f32), ot=vm(2, 256, 1024),
        top=vm(8, 1024, kind=f32), total=vm(8, 1024, kind=f32), back=vm(8, 1024, kind=f32), tops=vm(8, 8, 1024, kind=f32),
        gains=vm(8, 1024, kind=f32), mid=vm(128, 1024, kind=f32), g_acc=vm(128, 1024, kind=f32),
        gather_send=dma((16,)), gather_recv=dma((16,)),
        nt=vm(1024, 128, kind=f32), qxn=vm(2, 1024, 384), dt=vm(2, 256, 1024), dn=vm(2, 1024, 256),
        inner=vm(8, 1024, kind=f32), ds=vm(256, 1024), pf=vm(256, 1024), own=vm(128, 640, kind=f32), lg=vm(16, 128, 640),
        lg_send=dma((4, 2)), lg_recv=dma((16,)),
        gkr=vm(128, 128),
        at=vm(3, 3, 512, 256), at_send=vm(3, 3, 512, 128), at_sem=dma((2, 3, 3)),
        g=vm(3, JOBS, 256, W), g_send=dma((3, JOBS)), g_recv=dma((3, JOBS)),
        dense=vm(3, 4, 256, W), dense_send=vm(3, 4, 128, W), dense_sem=dma((2, 3)),
        d=vm(3, RING, 512, W), s1=vm(3, RING, 128, W, kind=f32), s2=vm(3, RING, 32, W, kind=f32),
        sum_send=dma((3, 6, 2, RING)), sum_recv=dma((3, 6, 2, RING)),
        **{
            side + name: vm(3, RING, 2, rows, width, kind=kind)
            for side in "sr"
            for name, rows, width, kind in (
                ("a", 128, W // 2, bf), ("b", 128, W, bf), ("c", 32, W // 2, bf),
                ("d", 32, W, bf), ("e", 8, W // 2, f32), ("f", 8, W, f32),
            )
        },
    )


def kernel(names, *refs):
    r = types.SimpleNamespace(**dict(zip(names, refs)))
    seq, h = lax.axis_index("seq"), lax.axis_index("head")
    me = place()
    load_first(r)
    barrier = pltpu.get_barrier_semaphore()
    peers = [(seq, (h + k) % 16) for k in range(1, 16)] + [other_core(me), beside(me, "y", 1), beside(me, "y", -1)]
    for peer in peers:
        pl.semaphore_signal(barrier, inc=1, device_id=peer, device_id_type=MESH)
    pl.semaphore_wait(barrier, len(peers))
    project(r, seq, h)
    r.nt[...] = r.cot[...].astype(f32).T
    choose_rows(r, me, 2, FEED)
    r.nt[...] = r.n1[...].astype(f32).T
    for order in range(3):
        choose_rows(r, me, order, ONE)
    attend(r, seq, h)
    r.nt[...] = r.attt[...].astype(f32)
    for order in (1, 2):
        choose_rows(r, me, order, OUT)

    def each(j, grad_gate, grad_up, act):
        for order, value in enumerate((grad_gate, grad_up, act)):
            give(r, me, order, j, value)
        sum_slot(r, me, j)

    def begin():
        r.nt[...] = r.n2[...].astype(f32).T
        for order in (0, 1):
            choose_rows(r, me, order, FEED)
        wait_rows(r, me, FEED)

    feed(r, begin, each)
    load_first(r, again=True)
    for c in range(2):
        give(r, me, 1, 11 + c, r.gb[:, c * 256 : (c + 1) * 256])
        give(r, me, 2, 11 + c, r.gb[:, 512 + c * 256 : 768 + c * 256])
    give_heads(r, me, 0, r.ga, r.ot)
    wait_rows(r, me, OUT)
    sum_slot(r, me, 11)
    prepare_back(r)

    @pl.loop(0, 8)
    def _(b):
        @pl.when(b <= h // 2)
        def _():
            back_step(r, seq, h, b)

        sum_slot(r, me, 12 + b)

    wait_rows(r, me, ONE)
    finish_queries(r, me)
    sum_slot(r, me, 1, True)
    finish_latent(r, me, seq, h)
    sum_slot(r, me, 2, True)
    for i in range(4):
        wait_first(r, i)
    finish_input(r)
    finish_rope(r, me)

    @pl.loop(3, 11)
    def _(t):
        sum_slot(r, me, t, True)

    sum_end(r, me)
    back_end(r, seq, h)
    for k in range(1, 16):
        @pl.when(h + k < 16)
        def _():
            ref = r.lx.at[h // 2, rows_of(h)]
            remote(ref, ref, r.gather_send.at[k], r.gather_recv.at[h], (seq, h)).wait_send()


def run(layer_input, second_start, mixer_gain, w_query, w_query_rope, w_latent, w_key_rope, w_key_up, w_value_up, w_out, feed_gain, w_gate, w_up, w_down, cotangent):
    freq = jnp.broadcast_to((10000.0 ** (-jnp.arange(16, dtype=f32) * 2.0 / 32))[:, None], (16, 128))
    args = dict(x=layer_input, cot=cotangent, second=second_start, gain1=mixer_gain[None], gain2=feed_gain[None], freq=freq,
        wkr=w_key_rope.T, kup=w_key_up, vup=w_value_up, wq=w_query, wqr=w_query_rope, wl=w_latent, wo_hbm=w_out, wg=w_gate, wu=w_up, wd=w_down)
    V, A, S = (pl.BlockSpec(memory_space=m) for m in (pltpu.VMEM, pl.ANY, pltpu.SMEM))
    specs = {n: V for n in INPUTS}
    specs["second"] = S
    for n in ("wq", "wqr", "wl", "wo_hbm", "wg", "wu", "wd"):
        specs[n] = A
    outs = dict(output=((128, 1024), bf), grad_input=((128, 1024), f32), sums=((3, 8, JOBS * W), f32))
    sc = scratch()
    names = INPUTS + tuple(outs) + tuple(sc)
    output, grad_input, sums = pl.pallas_call(
        lambda *refs: kernel(names, *refs),
        out_shape=[jax.ShapeDtypeStruct(*o) for o in outs.values()],
        in_specs=[specs[n] for n in INPUTS], out_specs=[V] * len(outs),
        scratch_shapes=list(sc.values()),
        compiler_params=pltpu.CompilerParams(collective_id=0, has_side_effects=True, vmem_limit_bytes=66900000),
        name="layer",
    )(*[args[n] for n in INPUTS])

    first, second, third = sums[0], sums[1], sums[2]

    def heads(block):
        return block.reshape(2, 4, 256).transpose(0, 2, 1)

    rope = first[:, 3840:]
    return (
        output,
        grad_input,
        rope[:, 32],
        jnp.concatenate([second[:, 3328:], third[:, 3328:3584]], 1),
        first[:, 3328:3840],
        third[:, 3584:],
        rope[:, :32],
        heads(first[:, 3072:3328]),
        heads(first[:, 2816:3072]),
        jnp.concatenate([second[:, 2816:3328], third[:, 2816:3328]], 1),
        rope[:, 33],
        first[:, :2816],
        second[:, :2816],
        third[:, :2816].T,
    )


def solution(mesh):
    in_specs = (
        P(("seq", "head"), None),
        P("seq"),
        P(),
        P(),
        P(),
        P(),
        P(),
        P(),
        P(),
        P(),
        P(),
        P(),
        P(),
        P(),
        P(("seq", "head"), None),
    )
    out_specs = (
        P(("seq", "head"), None),
        P(("seq", "head"), None),
        P(("seq", "head")),
        P(("seq", "head"), None),
        P(("seq", "head"), None),
        P(("seq", "head"), None),
        P(("seq", "head"), None),
        P(None, None, ("seq", "head")),
        P(None, None, ("seq", "head")),
        P(("seq", "head"), None),
        P(("seq", "head")),
        P(("seq", "head"), None),
        P(("seq", "head"), None),
        P(None, ("seq", "head")),
    )
    return jax.shard_map(run, mesh=mesh, in_specs=in_specs, out_specs=out_specs, check_vma=False)
```

time: 5040 us -> 238 us (0.05)
  waiting for transfers between devices: 4630 us -> 0 us
  Pallas kernels: 0 us -> 222 us
  matrix products: 145 us -> 0 us
  blocking collectives: 65.5 us -> 0 us
  other arithmetic: 63.2 us -> 0.64 us
  local copies, waits for them, and re-layouts: 75.2 us -> 13.5 us
    reduce_scatter x7 -> x0, waiting for transfers between devices: 4540 us -> none  [the longest x1 661 us: body(): lax.psum_scatter(grad_wup, ('seq', 'head'), scatter_dimension=0, tiled=True)]
    pallas_call x0 -> x1, Pallas kernels: none -> 222 us  [run(): pl.pallas_call(lambda *refs: kernel(names, *refs), out_shape=[jax.ShapeDt...]
    dot_general x74 -> x0, matrix products: 145 us -> none  [the longest x10 30.8 us: across(): lax.dot_general(left, right, (((0,), (0,)), ((), ())), preferred_element_...]
    unnamed x1 -> x0, blocking collectives: 65.5 us -> none
  transfers between devices with their start and end apart: 14 -> 0, of which waited for: 13 -> 0; matrix products, arithmetic and copies ran while one was open for 2% -> 0% of each run, Pallas kernels for 0% -> 0%
where the time goes in v2:
time: 238 us; the launch traced here: 237 us
  Pallas kernels  222 us (93%)
  local copies, waits for them, and re-layouts  13.5 us (6%)
    pallas_call x1, Pallas kernels, run(): pl.pallas_call(lambda *refs: kernel(names, *refs), out_shape=[jax.ShapeDt...  222 us

profile of v2, /device:TPU:0, one launch (start us, length us, event | category | flops | bytes accessed | tf_op | source)
XLA Modules:
  0.0 237.2 jit_solution(2538314077485683317)
XLA Ops:
  1.3 1.3 broadcast_in_dim.12.refs_3_
  2.6 1.3 broadcast_in_dim.13.refs_4_
  3.9 0.7 broadcast_in_dim.14.refs_5_
  4.5 221.7 %layer.1 = (bf16[128,1024]{1,0:T(8,128)(2,1)}, f32[128,1024]{1,0:T(8,128)}, f32[3,8,4096]{2,1,0:T(8,128)}) custom-call(bf16[128,1024]{1,0:T(8,128)(2,1)} %refs_0_.1, bf16[128,1024]{1,0:T(8,128)(2,1)} %refs_1_.1, s32[1]{0:T(128)S(6)} %copy.31.refs_2_, bf16[1,1024]{1,0:T(2,128)(2,1)} %broadcast_in_dim.12.refs_3_, bf16[1,1024]{1,0:T(2,128)(2,1)} %broadcast_in_dim.13.refs_4_, ...), custom_call_target="tpu_custom_call" | custom-call | tf_op jit(solution)/shard_map/layer/pallas_call | solution.py:735
  226.3 1.1 slice_bitcast_fusion.1
  227.4 0.7 slice_reduce_fusion
  228.1 0.6 slice.77
  228.7 0.6 slice.75
  229.3 0.6 slice.83
  229.9 0.6 reshape.41
  230.5 0.6 reshape.40
  231.1 0.6 slice.84
  231.8 0.6 fusion
  232.4 0.6 slice_bitcast_fusion.3
  233.0 0.6 pad_maximum_fusion
  233.7 1.7 copy.32
  235.3 1.9 copy.33
  (5 shorter events, 0.0 us)

commit v3 on v2

--- a/solution.py
+++ b/solution.py
@@ -12,8 +12,10 @@
 bf, f32 = jnp.bfloat16, jnp.float32
 W = 256
 EPS = 1e-6
+RATES = [float(v) for v in 10000.0 ** (-np.arange(16) * 2.0 / 32)]
 SCALE = 1.0 / math.sqrt(96)
 DEPTH = 4
+FEATURES, SPLIT = 560, 288
 
 
 def dot(a, b, ca=1, cb=0):
@@ -75,34 +77,34 @@
 def project(r, seq, h):
     x = r.x[...].astype(f32)
     inverse = lax.rsqrt(jnp.mean(x * x, -1, keepdims=True) + EPS)
-    n1 = (x * inverse * r.gain1[...].astype(f32)).astype(bf)
+    n1 = (x * inverse * r.gain1[...].astype(f32)[None]).astype(bf)
     r.n1[...] = n1
     bound = r.second[0]
     token = h * 128 + lax.broadcasted_iota(jnp.int32, (16, 128), 1)
     position = token - jnp.where(token >= bound, bound, 0)
-    angle = position.astype(f32) * r.freq[...]
+    step = lax.broadcasted_iota(jnp.int32, (16, 128), 0)
+    rate = jnp.ones((16, 128), f32)
+    for i in range(1, 16):
+        rate = jnp.where(step == i, RATES[i], rate)
+    angle = position.astype(f32) * rate
     cosine, sine = jnp.cos(angle), jnp.sin(angle)
     r.cos[...], r.sin[...] = cosine, sine
     wait_first(r, 3)
     lat = dot(n1, r.pool[3]).astype(bf)
     kr = turn(dot(r.wkr[...], n1, 1, 1), cosine, sine)
     flag = jnp.where(h == 15, 0.0, 1.0)
-    flags = jnp.where(lax.broadcasted_iota(jnp.int32, (96, 128), 0) == 0, flag, 0.0)
-    own = jnp.concatenate([kr, flags], 0).T.astype(bf)
-    b = h // 2
-    mine = r.lx.at[b, rows_of(h)]
-    mine[:, 0:256] = lat[:, 0:256]
-    mine[:, 256:384] = own
-    mine[:, 384:640] = lat[:, 256:512]
+    flags = jnp.where(lax.broadcasted_iota(jnp.int32, (16, 128), 0) == 0, flag, 0.0)
+    latt = lat.T
+    mine = r.lxt.at[h // 2, :, lanes((h % 2) * 128, 128)]
+    mine[0:256] = latt[0:256]
+    mine[256:304] = jnp.concatenate([kr, flags], 0).astype(bf)
+    mine[304:560] = latt[256:512]
 
     @pl.when(h % 2 == 0)
     def _():
-        r.lx[b, 128:256] = jnp.zeros((128, 640), bf)
-
-    for k in range(1, 16):
-        @pl.when(h + k < 16)
-        def _():
-            remote(mine, mine, r.gather_send.at[k], r.gather_recv.at[h], (seq, h + k)).start()
+        r.lxt[h // 2, SPLIT:FEATURES, 128:256] = jnp.zeros((FEATURES - SPLIT, 128), bf)
+
+    gather_first(r, seq, h)
 
     for i in range(2):
         wait_first(r, i)
@@ -129,49 +131,111 @@
             ).astype(bf)
 
 
+def latent_half(r, i, half):
+    rows = slice(0, SPLIT) if half == 0 else slice(SPLIT, FEATURES)
+    return r.lxt.at[i // 2, rows, lanes((i % 2) * 128, 128)]
+
+
+def gather_copy(r, seq, i, half, send, to):
+    ref = latent_half(r, i, half)
+    return remote(ref, ref, send, r.gather_recv.at[half, i], (seq, to))
+
+
+def first_targets(r, seq, h):
+    z, x = h // 4, h % 4
+    for k in range(1, 4):
+        there = (z + k) % 4
+        yield True, gather_copy(r, seq, h, 0, r.gather_send.at[0, k], z * 4 + (x + k) % 4)
+        yield there > z, gather_copy(r, seq, h, 1, r.gather_send.at[1, k], there * 4 + x)
+
+
+def second_targets(r, seq, h):
+    z, x = h // 4, h % 4
+    for j in range(4):
+        i = z * 4 + (x + j) % 4
+        sends = []
+        for k in range(1, 4):
+            there = (z + k) % 4
+            sends.append((there > z, gather_copy(r, seq, i, 0, r.gather_send.at[2 + j, k], there * 4 + x)))
+        yield (j > 0), gather_copy(r, seq, i, 0, r.gather_send.at[0, 0], h), sends
+        row = (z + 4 - j) % 4
+        i = row * 4 + x
+        sends = []
+        for k in range(1, 4):
+            there = (x + k) % 4
+            sends.append(((row < z) | ((row == z) & (there > x)), gather_copy(r, seq, i, 1, r.gather_send.at[6 + j, k], z * 4 + there)))
+        yield (row < z), gather_copy(r, seq, i, 1, r.gather_send.at[0, 0], h), sends
+
+
+def gather_first(r, seq, h):
+    for use, copy in first_targets(r, seq, h):
+        pl.when(use)(copy.start)
+
+
+def gather_second(r, seq, h):
+    for use, copy, sends in second_targets(r, seq, h):
+        pl.when(use)(copy.wait_recv)
+        for wanted, send in sends:
+            pl.when(wanted)(send.start)
+
+
+def gather_sent(r, seq, h):
+    for use, copy in first_targets(r, seq, h):
+        pl.when(use)(copy.wait_send)
+    for _, _, sends in second_targets(r, seq, h):
+        for wanted, send in sends:
+            pl.when(wanted)(send.wait_send)
+
+
 def gather_wait(r, seq, h, i):
-    ref = r.lx.at[i // 2, rows_of(i)]
-
-    @pl.when(i < h)
-    def _():
-        remote(ref, ref, r.gather_send.at[0], r.gather_recv.at[i], (seq, 0)).wait_recv()
+    pl.when((i < h) & (i // 4 != h // 4))(gather_copy(r, seq, i, 0, r.gather_send.at[0, 0], h).wait_recv)
+    pl.when((i < h) & (i % 4 != h % 4))(gather_copy(r, seq, i, 1, r.gather_send.at[0, 0], h).wait_recv)
+
+
+def load_latents(r, b):
+    r.lx[:, 0:256] = r.lxt[b, 0:256].T
+    r.lx[:, 256:384] = jnp.concatenate([r.lxt[b, 256:304], jnp.zeros((80, 256), bf)], 0).T
+    r.lx[:, 384:640] = r.lxt[b, 304:560].T
 
 
 def attend_step(r, seq, h, b, diag):
     gather_wait(r, seq, h, 2 * b)
     gather_wait(r, seq, h, 2 * b + 1)
-    r.lxt[...] = r.lx[b].T
+    load_latents(r, b)
+    wide = 512
+    units = [(g, slice(c * wide, (c + 1) * wide)) for g in range(2) for c in range(1024 // wide)]
+    scores = [dot(r.lx[:, g * 256 : g * 256 + 384], r.qxt[g, :, cols]) for g, cols in units]
     if diag:
         bound = r.second[0]
         key = b * 256 + lax.broadcasted_iota(jnp.int32, (256, 128), 0)
         row = h * 128 + lax.broadcasted_iota(jnp.int32, (256, 128), 1)
         ok = (key <= row) & ((key >= bound) == (row >= bound))
-        mask = jnp.where(ok, 0.0, 1.0)
-        mask = jnp.concatenate([mask, mask], 1)
-    for g in range(2):
-        at = 0 if g == 0 else 384
-        for c in range(4):
-            cols = slice(c * 256, (c + 1) * 256)
-            s = dot(r.lx[b, :, g * 256 : g * 256 + 384], r.qxt[g, :, cols])
-            if diag:
-                s = jnp.where(mask > 0.5, -1e30, s)
-            top = jnp.max(s, 0, keepdims=True)
-            if not diag:
-                before = r.top[g : g + 1, cols]
-                top = jnp.maximum(top, before)
-            p = jnp.exp(s - top)
-            total = jnp.sum(p, 0, keepdims=True)
-            pb = p.astype(bf)
-            r.p[b, g, :, cols] = pb
-            o = dot(r.lxt[at : at + 256], pb)
-            if not diag:
-                fade = jnp.exp(before - top)
-                total = total + r.total[g : g + 1, cols] * fade
-                o = o + r.acc[g, 0:256, cols] * fade
-            r.acc[g, 0:256, cols] = o
-            r.total[g : g + 1, cols] = total
-            r.top[g : g + 1, cols] = top
-            r.tops[b, g : g + 1, cols] = top
+        barred = jnp.where(ok, 0.0, 1.0)
+        barred = jnp.concatenate([barred] * (wide // 128), 1)
+    kept = []
+    for (g, cols), s in zip(units, scores):
+        if diag:
+            s = jnp.where(barred > 0.5, -1e30, s)
+        top = jnp.max(s, 0, keepdims=True)
+        fade = None
+        if not diag:
+            before = r.top[g : g + 1, cols]
+            top = jnp.maximum(top, before)
+            fade = jnp.exp(before - top)
+        p = jnp.exp(s - top)
+        total = jnp.sum(p, 0, keepdims=True)
+        if not diag:
+            total = total + r.total[g : g + 1, cols] * fade
+        p = p.astype(bf)
+        r.p[b, g, :, cols] = p
+        r.total[g : g + 1, cols] = total
+        r.top[g : g + 1, cols] = top
+        r.tops[pl.ds(b * 2 + g, 1), cols] = top
+        kept.append((p, fade))
+    for (g, cols), (p, fade) in zip(units, kept):
+        at = 0 if g == 0 else 304
+        o = dot(r.lxt[b, at : at + 256], p)
+        r.acc[g, 0:256, cols] = o if diag else o + r.acc[g, 0:256, cols] * fade
 
 
 def attend(r, seq, h):
@@ -191,15 +255,14 @@
             r.attt[head * 64 : (head + 1) * 64] = dot(
                 r.vt[g, e * 64 : (e + 1) * 64], r.ot[g, :, e * 128 : (e + 1) * 128]
             ).astype(bf)
-    r.att[...] = r.attt[...].T
 
 
 def feed(r, begin, each):
     wait_first(r, 4)
-    r.mid[...] = r.x[...].astype(f32) + dot(r.att[...], r.wo[...])
+    r.mid[...] = r.x[...].astype(f32) + dot(r.attt[...].T, r.wo[...])
     mid = r.mid[...]
     inverse = lax.rsqrt(jnp.mean(mid * mid, -1, keepdims=True) + EPS)
-    gain = r.gain2[...].astype(f32)
+    gain = r.gain2[...].astype(f32)[None]
     r.n2[...] = (mid * inverse * gain).astype(bf)
     r.grad_input[...] = mid
     r.g_acc[...] = jnp.zeros((128, 1024), f32)
@@ -211,16 +274,18 @@
         for copy in chunk_copies(r, j):
             copy.wait()
         n2, cot = r.n2[...], r.cot[...]
-        gate = dot(n2, r.pool[slot, :, 0:W])
-        up = dot(n2, r.pool[slot, :, W : 2 * W])
+        both = dot(n2, r.pool[slot])
         grad = dot(cot, r.wdpool[slot], 1, 1)
+        gate, up = both[:, :W], both[:, W:]
         sigma = jax.nn.sigmoid(gate)
         swish = gate * sigma
         act = (swish * up).astype(bf)
         grad_gate = (grad * up * sigma * (1.0 + gate * (1.0 - sigma))).astype(bf)
         grad_up = (grad * swish).astype(bf)
-        r.grad_input[...] += dot(act, r.wdpool[slot])
-        r.g_acc[...] += dot(grad_gate, r.pool[slot, :, 0:W], 1, 1) + dot(grad_up, r.pool[slot, :, W : 2 * W], 1, 1)
+        out = dot(act, r.wdpool[slot])
+        back = dot(jnp.concatenate([grad_gate, grad_up], 1), r.pool[slot], 1, 1)
+        r.grad_input[...] += out
+        r.g_acc[...] += back
 
         @pl.when(j + DEPTH < 11)
         def _():
@@ -243,7 +308,6 @@
 
 RING = 4
 ORDERS = (("y", "z", "x"), ("z", "x", "y"), ("x", "y", "z"))
-EARLY = (12, 13, 13)
 JOBS = 16
 FEED, OUT, ONE = 0, 1, 2
 PHASES = ("a", "b", "c", "d", "e", "f")
@@ -385,7 +449,7 @@
     return get
 
 
-def products(r, me, order, job, late):
+def products(r, me, order, job):
     slot = job % RING
 
     def plain(which):
@@ -403,23 +467,19 @@
             r.d[order, slot, q * 128 : (q + 1) * 128] = dot(pick, r.dense[which, q]).astype(bf)
 
     if order == 0:
-        if late:
-            pl.when(job == 12)(lambda: thick(1))
-            pl.when((job == 13) | (job == 14))(lambda: plain(ONE))
-            pl.when(job == 15)(lambda: thick(2))
-        else:
-            pl.when(job < 11)(lambda: plain(FEED))
-            pl.when(job == 11)(lambda: thick(0))
-    elif late:
-        plain(ONE)
+        pl.when(job < 11)(lambda: plain(FEED))
+        pl.when(job == 11)(lambda: thick(0))
+        pl.when(job == 12)(lambda: thick(1))
+        pl.when((job == 13) | (job == 14))(lambda: plain(ONE))
+        pl.when(job == 15)(lambda: thick(2))
     else:
-        plain(jnp.where(job < 11, FEED, OUT))
-
-
-def sum_step(r, me, order, k, job, late):
+        plain(jnp.where(job < 11, FEED, jnp.where(job < 13, OUT, ONE)))
+
+
+def sum_step(r, me, order, k, job):
     get = block_of(r, me, order, min(k // 2, 2), job)
     if k == 0:
-        products(r, me, order, job, late)
+        products(r, me, order, job)
         first_half(r, me, order, 0, job, get(2))
     elif k % 2:
         second_half(r, me, order, k // 2, job, get)
@@ -434,16 +494,14 @@
         r.sums[order, :, lanes(job * W, W)] = total(r, me, order, 2, job, own)
 
 
-def sum_slot(r, me, t, late=False):
+def sum_slot(r, me, t):
     for k in reversed(range(7)):
-        for order in range(3):
-            base = EARLY[order] if late else 0
-            end = JOBS if late else EARLY[order]
-            job = base + t - 1 - k
-
-            @pl.when((job >= base) & (job < end))
-            def _():
-                sum_step(r, me, order, k, job, late)
+        job = t - 2 * k
+
+        @pl.when((job >= 0) & (job < JOBS))
+        def _():
+            for order in range(3):
+                sum_step(r, me, order, k, job)
 
 
 def sum_end(r, me):
@@ -478,72 +536,131 @@
             back = r.back[g : g + 1, cols]
             inner = jnp.sum(ga.astype(f32) * r.attt[head * 64 : (head + 1) * 64].astype(f32), 0, keepdims=True)
             r.inner[g : g + 1, cols] = inner * back
-            r.dt[g, :, cols] = (dot(r.vt[g, e * 64 : (e + 1) * 64, :], ga, 0, 0) * back).astype(bf)
-        r.dn[g] = r.dt[g].T
+            r.qxt[g, 0:256, cols] = (dot(r.vt[g, e * 64 : (e + 1) * 64, :], ga, 0, 0) * back).astype(bf)
+        r.dn[g] = r.qxt[g, 0:256].T
     r.acc[...] = jnp.zeros((2, 384, 1024), f32)
-
-
-def latent_copy(r, seq, h, b, s):
+    r.own_z[...] = jnp.zeros((4, SPLIT, 128), bf)
+
+
+def inward(r, seq, h, b, s, half):
+    z, x = h // 4, h % 4
+    row, column = b // 2, (2 * b + s) % 4
     slot = b % 4
-    return remote(
-        r.wdpool.at[slot, s * 128 : s * 128 + 128, 0:640], r.lg.at[h],
-        r.lg_send.at[slot, s], r.lg_recv.at[h], (seq, b * 2 + s),
-    )
+    cols = lanes(slot * 256 + s * 128, 128)
+    if half == 0:
+        src, step = r.wo.at[0:SPLIT, cols], (z - row + 3) % 4
+        copy = remote(src, r.in_z.at[step, column], r.in_send.at[slot, s, 0], r.in_z_recv.at[step, column], (seq, row * 4 + x))
+        return copy, row < z, (row == z) & (2 * b + s <= h)
+    src, step = r.wo.at[SPLIT:FEATURES, cols], (x - column + 3) % 4
+    copy = remote(src, r.in_x.at[step, row], r.in_send.at[slot, s, 1], r.in_x_recv.at[step, row], (seq, z * 4 + column))
+    return copy, (column != x) & (2 * b + s < h), (column == x) & (2 * b + s <= h)
 
 
 def back_step(r, seq, h, b):
     @pl.when(b >= 4)
     def _():
         for s in (0, 1):
-            latent_copy(r, seq, h, b - 4, s).wait_send()
-
-    slot = b % 4
-    r.lxt[...] = r.lx[b].T
-    rope = None
-    for g in range(2):
-        at = 0 if g == 0 else 384
-        for c in range(4):
-            cols = slice(c * 256, (c + 1) * 256)
-            fade = jnp.exp(r.tops[b, g : g + 1, cols] - r.top[g : g + 1, cols])
-            p = r.p[b, g, :, cols].astype(f32) * fade
-            dp = dot(r.lx[b, :, at : at + 256], r.dt[g, :, cols])
-            r.ds[:, cols] = (p * (dp - r.inner[g : g + 1, cols])).astype(bf)
-            r.pf[:, cols] = p.astype(bf)
-        ds = r.ds[...]
+            for half in (0, 1):
+                copy, sent, _ = inward(r, seq, h, b - 4, s, half)
+                pl.when(sent)(copy.wait_send)
+
+    load_latents(r, b)
+    cols = lanes((b % 4) * 256, 256)
+    for g, at in ((0, 0), (1, 384)):
+        dp = dot(r.lx[:, at : at + 256], r.qxt[g, 0:256])
+        p = r.p[b, g].astype(f32) * jnp.exp(r.tops[pl.ds(b * 2 + g, 1)] - r.top[g : g + 1])
+        ds = (p * (dp - r.inner[g : g + 1])).astype(bf)
         gl = dot(ds, r.qxn[g])
-        gp = dot(r.pf[...], r.dn[g])
-        r.acc[g] += dot(r.lxt[g * 256 : g * 256 + 384], ds)
+        gp = dot(p.astype(bf), r.dn[g])
+        r.acc[g, 0:304] += dot(r.lxt[b, g * 256 : g * 256 + 304], ds)
         if g == 0:
-            left = gl[:, 0:256] + gp
+            r.wo[0:256, cols] = (gl[:, 0:256] + gp).astype(bf).T
             rope = gl[:, 256:384]
         else:
-            rope = rope + gl[:, 0:128]
-            right = gl[:, 128:384] + gp
-    whole = jnp.concatenate([left, rope, right], 1)
-    r.wdpool[slot, :, 0:640] = whole.astype(bf)
+            r.wo[256:304, cols] = (rope + gl[:, 0:128]).astype(bf).T[0:48]
+            r.wo[304:560, cols] = (gl[:, 128:384] + gp).astype(bf).T
     for s in (0, 1):
-        @pl.when(2 * b + s < h)
-        def _():
-            latent_copy(r, seq, h, b, s).start()
-
-        @pl.when(2 * b + s == h)
-        def _():
-            r.own[...] = whole[s * 128 : s * 128 + 128]
-
-
-def back_end(r, seq, h):
+        for half in (0, 1):
+            copy, sent, stays = inward(r, seq, h, b, s, half)
+            pl.when(sent)(copy.start)
+
+            @pl.when(stays)
+            def _():
+                cols = lanes((b % 4) * 256 + s * 128, 128)
+                if half == 0:
+                    r.own_z[(2 * b + s) % 4] = r.wo[0:SPLIT, cols]
+                else:
+                    r.own_x[b // 2] = r.wo[SPLIT:FEATURES, cols]
+
+
+def back_sent(r, seq, h):
     last = h // 2
     for d in range(4):
         b = last - d
         for s in (0, 1):
-            @pl.when((b >= 0) & (2 * b + s < h))
+            for half in (0, 1):
+                copy, sent, _ = inward(r, seq, h, b, s, half)
+                pl.when((b >= 0) & sent)(copy.wait_send)
+
+
+def onward(r, seq, h, k, half):
+    z, x = h // 4, h % 4
+    if half == 0:
+        column = (x + k) % 4
+        copy = remote(r.out_x.at[k - 1], r.end_x.at[3 - k], r.out_send.at[0, k], r.end_recv.at[0, 3 - k], (seq, z * 4 + column))
+        return copy, (z < 3) | (column < x)
+    row = z - k
+    copy = remote(r.out_z.at[k - 1], r.end_z.at[k - 1], r.out_send.at[1, k], r.end_recv.at[1, k - 1], (seq, (row % 4) * 4 + x))
+    return copy, row >= 0
+
+
+def sum_latents(r, seq, h):
+    z, x = h // 4, h % 4
+    for k in range(4):
+        column = (x + k) % 4
+        r.nt[0:SPLIT] = jnp.where((column <= x), r.own_z[column].astype(f32), 0.0)
+        for step in range(3):
+            @pl.when(z + 1 + step < 4)
             def _():
-                latent_copy(r, seq, h, b, s).wait_send()
+                ref = r.in_z.at[step, column]
+                remote(ref, ref, r.in_send.at[0, 0, 0], r.in_z_recv.at[step, column], (seq, h)).wait_recv()
+                r.nt[0:SPLIT] += r.in_z[step, column].astype(f32)
+
+        if k == 0:
+            r.own[0:SPLIT] = r.nt[0:SPLIT]
+        else:
+            r.out_x[k - 1] = r.nt[0:SPLIT].astype(bf)
+            copy, sent = onward(r, seq, h, k, 0)
+            pl.when(sent)(copy.start)
+    for k in range(4):
+        @pl.when(z - k >= 0)
+        def _():
+            row = z - k
+            r.nt[SPLIT:FEATURES] = r.own_x[row].astype(f32)
+            for step in range(3):
+                @pl.when((k > 0) | ((x + 1 + step) % 4 > x))
+                def _():
+                    ref = r.in_x.at[step, row]
+                    remote(ref, ref, r.in_send.at[0, 0, 0], r.in_x_recv.at[step, row], (seq, h)).wait_recv()
+                    r.nt[SPLIT:FEATURES] += r.in_x[step, row].astype(f32)
+
+            if k == 0:
+                r.own[SPLIT:FEATURES] = r.nt[SPLIT:FEATURES]
+            else:
+                r.out_z[k - 1] = r.nt[SPLIT:FEATURES].astype(bf)
+                onward(r, seq, h, k, 1)[0].start()
+
+
+def latents_sent(r, seq, h):
+    for k in range(1, 4):
+        for half in (0, 1):
+            copy, sent = onward(r, seq, h, k, half)
+            pl.when(sent)(copy.wait_send)
 
 
 def finish_queries(r, me):
     for g in range(2):
-        at, rope = (0, 256) if g == 0 else (128, 0)
+        at, rope = (0, 256) if g == 0 else (48, 0)
         r.ot[g] = (r.acc[g, at : at + 256] * SCALE).astype(bf)
         for e in range(8):
             head = g * 8 + e
@@ -553,27 +670,34 @@
             r.nt[head * 32 : (head + 1) * 32] = turn(turned, r.cos[...], -r.sin[...])
     r.n2[...] = r.attt[...].T
     r.gb[:, 0:512] = r.nt[0:512].T.astype(bf)
-    for c in range(3):
+    for c in range(2):
         give(r, me, 1, 13 + c, r.n2[:, c * 256 : (c + 1) * 256])
-    give(r, me, 2, 13, r.n2[:, 768:1024])
+        give(r, me, 2, 13 + c, r.n2[:, 512 + c * 256 : 768 + c * 256])
     for c in range(2):
         give(r, me, 0, 13 + c, r.gb[:, c * 256 : (c + 1) * 256])
     give_heads(r, me, 1, r.qt, r.ot)
 
 
 def finish_latent(r, me, seq, h):
-    @pl.loop(0, 16)
-    def _(j):
-        @pl.when(j > h)
+    z, x = h // 4, h % 4
+    for k in range(3):
+        @pl.when((z < 3) | ((x + 1 + k) % 4 > x))
         def _():
-            remote(r.lg.at[j], r.lg.at[j], r.lg_send.at[0, 0], r.lg_recv.at[j], (seq, 0)).wait_recv()
-            r.own[...] += r.lg[j].astype(f32)
-
-    r.gb[:, 512:768] = r.own[:, 0:256].astype(bf)
-    r.gb[:, 768:1024] = r.own[:, 384:640].astype(bf)
-    for c in range(2):
-        give(r, me, 2, 14 + c, r.gb[:, 512 + c * 256 : 768 + c * 256])
-    turned = r.own[:, 256:384].astype(bf).astype(f32).T[0:32]
+            ref = r.end_x.at[k]
+            remote(ref, ref, r.out_send.at[0, 0], r.end_recv.at[0, k], (seq, h)).wait_recv()
+            r.own[0:SPLIT] += r.end_x[k].astype(f32)
+
+        @pl.when(z + 1 + k < 4)
+        def _():
+            ref = r.end_z.at[k]
+            remote(ref, ref, r.out_send.at[0, 0], r.end_recv.at[1, k], (seq, h)).wait_recv()
+            r.own[SPLIT:FEATURES] += r.end_z[k].astype(f32)
+
+    r.gb[:, 512:768] = r.own[0:256].T.astype(bf)
+    r.gb[:, 768:1024] = r.own[304:560].T.astype(bf)
+    give(r, me, 1, 15, r.gb[:, 512:768])
+    give(r, me, 2, 15, r.gb[:, 768:1024])
+    turned = r.own[256:288].astype(bf).astype(f32)
     kr = turn(turned, r.cos[...], -r.sin[...])
     r.gkr[...] = jnp.concatenate([kr, jnp.zeros((96, 128), f32)], 0).T.astype(bf)
 
@@ -586,7 +710,7 @@
     x = r.x[...].astype(f32)
     inverse = lax.rsqrt(jnp.mean(x * x, -1, keepdims=True) + EPS)
     r.gains[0:1] = jnp.sum(grad * x * inverse, 0, keepdims=True)
-    scaled = grad * r.gain1[...].astype(f32)
+    scaled = grad * r.gain1[...].astype(f32)[None]
     r.grad_input[...] = r.mid[...] + inverse * scaled - x * (inverse * inverse * inverse) * jnp.mean(x * scaled, -1, keepdims=True)
 
 
@@ -611,7 +735,7 @@
     dense_copy(r, me, 2).start()
 
 
-INPUTS = ("x", "cot", "second", "gain1", "gain2", "freq", "wkr", "kup", "vup", "wq", "wqr", "wl", "wo_hbm", "wg", "wu", "wd")
+INPUTS = ("x", "cot", "second", "gain1", "gain2", "wkr", "kup", "vup", "wq", "wqr", "wl", "wo_hbm", "wg", "wu", "wd")
 
 
 def scratch():
@@ -620,16 +744,18 @@
     return dict(
         pool=vm(4, 1024, 512), wdpool=vm(4, 256, 1024), wo=vm(1024, 1024),
         first_sem=dma((5,)), chunk_sem=dma((4, 3)),
-        n1=vm(128, 1024), n2=vm(128, 1024), gb=vm(128, 1024), ga=vm(1024, 128), att=vm(128, 1024), attt=vm(1024, 128),
+        n1=vm(128, 1024), n2=vm(128, 1024), gb=vm(128, 1024), ga=vm(1024, 128), attt=vm(1024, 128),
         cos=vm(16, 128, kind=f32), sin=vm(16, 128, kind=f32),
-        lx=vm(8, 256, 640), lxt=vm(640, 256), qt=vm(1024, 128), kt=vm(2, 512, 256), vt=vm(2, 512, 256),
+        lx=vm(256, 640), lxt=vm(8, FEATURES, 256), qt=vm(1024, 128), kt=vm(2, 512, 256), vt=vm(2, 512, 256),
         qxt=vm(2, 384, 1024), p=vm(8, 2, 256, 1024), acc=vm(2, 384, 1024, kind=f32), ot=vm(2, 256, 1024),
-        top=vm(8, 1024, kind=f32), total=vm(8, 1024, kind=f32), back=vm(8, 1024, kind=f32), tops=vm(8, 8, 1024, kind=f32),
+        top=vm(8, 1024, kind=f32), total=vm(8, 1024, kind=f32), back=vm(8, 1024, kind=f32), tops=vm(16, 1024, kind=f32),
         gains=vm(8, 1024, kind=f32), mid=vm(128, 1024, kind=f32), g_acc=vm(128, 1024, kind=f32),
-        gather_send=dma((16,)), gather_recv=dma((16,)),
-        nt=vm(1024, 128, kind=f32), qxn=vm(2, 1024, 384), dt=vm(2, 256, 1024), dn=vm(2, 1024, 256),
-        inner=vm(8, 1024, kind=f32), ds=vm(256, 1024), pf=vm(256, 1024), own=vm(128, 640, kind=f32), lg=vm(16, 128, 640),
-        lg_send=dma((4, 2)), lg_recv=dma((16,)),
+        gather_send=dma((10, 4)), gather_recv=dma((2, 16)),
+        nt=vm(1024, 128, kind=f32), qxn=vm(2, 1024, 384), dn=vm(2, 1024, 256),
+        inner=vm(8, 1024, kind=f32), own=vm(FEATURES, 128, kind=f32),
+        in_z=vm(3, 4, SPLIT, 128), in_x=vm(3, 4, FEATURES - SPLIT, 128), own_z=vm(4, SPLIT, 128), own_x=vm(4, FEATURES - SPLIT, 128),
+        out_x=vm(3, SPLIT, 128), out_z=vm(3, FEATURES - SPLIT, 128), end_x=vm(3, SPLIT, 128), end_z=vm(3, FEATURES - SPLIT, 128),
+        in_send=dma((4, 2, 2)), in_z_recv=dma((3, 4)), in_x_recv=dma((3, 4)), out_send=dma((2, 4)), end_recv=dma((2, 3)),
         gkr=vm(128, 128),
         at=vm(3, 3, 512, 256), at_send=vm(3, 3, 512, 128), at_sem=dma((2, 3, 3)),
         g=vm(3, JOBS, 256, W), g_send=dma((3, JOBS)), g_recv=dma((3, JOBS)),
@@ -658,6 +784,7 @@
         pl.semaphore_signal(barrier, inc=1, device_id=peer, device_id_type=MESH)
     pl.semaphore_wait(barrier, len(peers))
     project(r, seq, h)
+    gather_second(r, seq, h)
     r.nt[...] = r.cot[...].astype(f32).T
     choose_rows(r, me, 2, FEED)
     r.nt[...] = r.n1[...].astype(f32).T
@@ -668,16 +795,22 @@
     for order in (1, 2):
         choose_rows(r, me, order, OUT)
 
-    def each(j, grad_gate, grad_up, act):
-        for order, value in enumerate((grad_gate, grad_up, act)):
-            give(r, me, order, j, value)
-        sum_slot(r, me, j)
-
     def begin():
         r.nt[...] = r.n2[...].astype(f32).T
         for order in (0, 1):
             choose_rows(r, me, order, FEED)
-        wait_rows(r, me, FEED)
+
+    def each(j, grad_gate, grad_up, act):
+        for order, value in enumerate((grad_gate, grad_up, act)):
+            give(r, me, order, j, value)
+
+        @pl.when(j % 2 == 1)
+        def _():
+            @pl.when(j == 1)
+            def _():
+                wait_rows(r, me, FEED)
+
+            sum_slot(r, me, j // 2)
 
     feed(r, begin, each)
     load_first(r, again=True)
@@ -685,9 +818,8 @@
         give(r, me, 1, 11 + c, r.gb[:, c * 256 : (c + 1) * 256])
         give(r, me, 2, 11 + c, r.gb[:, 512 + c * 256 : 768 + c * 256])
     give_heads(r, me, 0, r.ga, r.ot)
+    prepare_back(r)
     wait_rows(r, me, OUT)
-    sum_slot(r, me, 11)
-    prepare_back(r)
 
     @pl.loop(0, 8)
     def _(b):
@@ -695,34 +827,34 @@
         def _():
             back_step(r, seq, h, b)
 
-        sum_slot(r, me, 12 + b)
-
+        @pl.when(b < 7)
+        def _():
+            sum_slot(r, me, 5 + b)
+
+    finish_queries(r, me)
     wait_rows(r, me, ONE)
-    finish_queries(r, me)
-    sum_slot(r, me, 1, True)
+    sum_slot(r, me, 12)
+    sum_latents(r, seq, h)
+    sum_slot(r, me, 13)
+    sum_slot(r, me, 14)
     finish_latent(r, me, seq, h)
-    sum_slot(r, me, 2, True)
     for i in range(4):
         wait_first(r, i)
     finish_input(r)
     finish_rope(r, me)
 
-    @pl.loop(3, 11)
+    @pl.loop(15, 28)
     def _(t):
-        sum_slot(r, me, t, True)
+        sum_slot(r, me, t)
 
     sum_end(r, me)
-    back_end(r, seq, h)
-    for k in range(1, 16):
-        @pl.when(h + k < 16)
-        def _():
-            ref = r.lx.at[h // 2, rows_of(h)]
-            remote(ref, ref, r.gather_send.at[k], r.gather_recv.at[h], (seq, h)).wait_send()
+    back_sent(r, seq, h)
+    latents_sent(r, seq, h)
+    gather_sent(r, seq, h)
 
 
 def run(layer_input, second_start, mixer_gain, w_query, w_query_rope, w_latent, w_key_rope, w_key_up, w_value_up, w_out, feed_gain, w_gate, w_up, w_down, cotangent):
-    freq = jnp.broadcast_to((10000.0 ** (-jnp.arange(16, dtype=f32) * 2.0 / 32))[:, None], (16, 128))
-    args = dict(x=layer_input, cot=cotangent, second=second_start, gain1=mixer_gain[None], gain2=feed_gain[None], freq=freq,
+    args = dict(x=layer_input, cot=cotangent, second=second_start, gain1=mixer_gain, gain2=feed_gain,
         wkr=w_key_rope.T, kup=w_key_up, vup=w_value_up, wq=w_query, wqr=w_query_rope, wl=w_latent, wo_hbm=w_out, wg=w_gate, wu=w_up, wd=w_down)
     V, A, S = (pl.BlockSpec(memory_space=m) for m in (pltpu.VMEM, pl.ANY, pltpu.SMEM))
     specs = {n: V for n in INPUTS}
@@ -741,28 +873,47 @@
         name="layer",
     )(*[args[n] for n in INPUTS])
 
-    first, second, third = sums[0], sums[1], sums[2]
-
-    def heads(block):
-        return block.reshape(2, 4, 256).transpose(0, 2, 1)
-
-    rope = first[:, 3840:]
-    return (
-        output,
-        grad_input,
-        rope[:, 32],
-        jnp.concatenate([second[:, 3328:], third[:, 3328:3584]], 1),
-        first[:, 3328:3840],
-        third[:, 3584:],
-        rope[:, :32],
-        heads(first[:, 3072:3328]),
-        heads(first[:, 2816:3072]),
-        jnp.concatenate([second[:, 2816:3328], third[:, 2816:3328]], 1),
-        rope[:, 33],
-        first[:, :2816],
-        second[:, :2816],
-        third[:, :2816].T,
-    )
+    return place_results(output, grad_input, sums)
+
+
+def place_kernel(output, grad_input, sums, *outs):
+    first, second, third = (sums.at[i] for i in range(3))
+    outs[0][...] = output[...]
+    outs[1][...] = grad_input[...]
+    rope = first[:, 3840:3968]
+    turned = jnp.concatenate([rope, jnp.zeros((120, 128), f32)], 0).T
+    outs[2][...] = turned[32:33, 0:8]
+    outs[3][:, 0:512] = second[:, 3328:3840]
+    outs[3][:, 512:1024] = third[:, 3328:3840]
+    outs[4][...] = first[:, 3328:3840]
+    outs[5][:, 0:256] = second[:, 3840:4096]
+    outs[5][:, 256:512] = third[:, 3840:4096]
+    outs[6][...] = rope[:, 0:32]
+    for g in range(2):
+        outs[7][g] = first[g * 4 : g * 4 + 4, 3072:3328]
+        outs[8][g] = first[g * 4 : g * 4 + 4, 2816:3072]
+    outs[9][:, 0:512] = second[:, 2816:3328]
+    outs[9][:, 512:1024] = third[:, 2816:3328]
+    outs[10][...] = turned[33:34, 0:8]
+    outs[11][...] = first[:, 0:2816]
+    outs[12][...] = second[:, 0:2816]
+    outs[13][...] = third[:, 0:2816]
+
+
+def place_results(output, grad_input, sums):
+    shapes = [(1, 8), (8, 1024), (8, 512), (8, 512), (8, 32), (2, 4, 256), (2, 4, 256), (8, 1024), (1, 8), (8, 2816), (8, 2816), (8, 2816)]
+    outs = list(pl.pallas_call(
+        place_kernel,
+        out_shape=[jax.ShapeDtypeStruct((128, 1024), bf), jax.ShapeDtypeStruct((128, 1024), f32)]
+        + [jax.ShapeDtypeStruct(shape, f32) for shape in shapes],
+        name="place",
+    )(output, grad_input, sums))
+    for i in (2, 10):
+        outs[i] = outs[i].reshape(8)
+    for i in (7, 8):
+        outs[i] = outs[i].transpose(0, 2, 1)
+    outs[13] = outs[13].T
+    return tuple(outs)
 
 
 def solution(mesh):

time: 238 us -> 131 us (0.55)
  Pallas kernels: 222 us -> 130 us
  local copies, waits for them, and re-layouts: 13.5 us -> 0 us
    pallas_call x1, Pallas kernels: 222 us -> 127 us  [run(): pl.pallas_call(lambda *refs: kernel(names, *refs), out_shape=[jax.ShapeDt...]
    slice x10 -> x0, local copies, waits for them, and re-layouts: 3.83 us -> none  [the longest x1 0.73 us: run(): rope[:, 33]]
    unnamed x2 -> x0, local copies, waits for them, and re-layouts: 3.55 us -> none
    broadcast_in_dim x3 -> x0, local copies, waits for them, and re-layouts: 3.22 us -> none  [the longest x1 1.28 us: run(): mixer_gain[None]]
where the time goes in v3:
time: 131 us
  Pallas kernels  130 us (99%)
  between operations  1.43 us (1%)
    pallas_call x1, Pallas kernels, run(): pl.pallas_call(lambda *refs: kernel(names, *refs), out_shape=[jax.ShapeDt...  127 us

profile of v3, /device:TPU:0, one launch (start us, length us, event | category | flops | bytes accessed | tf_op | source)
XLA Modules:
  0.0 131.0 jit_solution(10690234392088849859)
XLA Ops:
  1.3 127.3 %layer.1 = (bf16[128,1024]{1,0:T(8,128)(2,1)}, f32[128,1024]{1,0:T(8,128)}, f32[3,8,4096]{2,1,0:T(8,128)}) custom-call(bf16[128,1024]{1,0:T(8,128)(2,1)} %refs_0_.1, bf16[128,1024]{1,0:T(8,128)(2,1)} %refs_1_.1, s32[1]{0:T(128)S(6)} %copy.29.refs_2_, bf16[1024]{0:T(1024)(128)(2,1)} %refs_3_.1, bf16[1024]{0:T(1024)(128)(2,1)} %refs_4_.1, ...), custom_call_target="tpu_custom_call" | custom-call | tf_op jit(solution)/shard_map/layer/pallas_call | solution.py:867
  128.6 2.3 %place.1 = (bf16[128,1024]{1,0:T(8,128)(2,1)}, f32[128,1024]{1,0:T(8,128)}, f32[1,8]{1,0:T(1,128)}, f32[8,1024]{1,0:T(8,128)}, f32[8,512]{1,0:T(8,128)}, /*index...) custom-call(bf16[128,1024]{1,0:T(8,128)(2,1)} %get-tuple-element.31., ...), custom_call_target="tpu_custom_call" | custom-call | tf_op jit(solution)/shard_map/place/pallas_call | solution.py:905

commit v4 on v3

--- a/solution.py
+++ b/solution.py
@@ -50,7 +50,18 @@
     return jnp.concatenate([first * cosine - second * sine, first * sine + second * cosine], -2)
 
 
+def small_copy(r, name):
+    return pltpu.make_async_copy(getattr(r, name + "_hbm"), getattr(r, name), r.small_sem.at[SMALL.index(name)])
+
+
+def result_copy(r, name):
+    return pltpu.make_async_copy(getattr(r, name), getattr(r, name + "_hbm"), r.result_sem.at[RESULTS.index(name)])
+
+
 def load_first(r, again=False):
+    if not again:
+        for name in SMALL:
+            small_copy(r, name).start()
     for i in range(2):
         pltpu.make_async_copy(r.wq.at[:, i * 512 : (i + 1) * 512], r.pool.at[i], r.first_sem.at[i]).start()
     pltpu.make_async_copy(r.wqr, r.pool.at[2], r.first_sem.at[2]).start()
@@ -75,6 +86,8 @@
 
 
 def project(r, seq, h):
+    for name in ("x", "gain1", "wkr"):
+        small_copy(r, name).wait()
     x = r.x[...].astype(f32)
     inverse = lax.rsqrt(jnp.mean(x * x, -1, keepdims=True) + EPS)
     n1 = (x * inverse * r.gain1[...].astype(f32)[None]).astype(bf)
@@ -116,9 +129,10 @@
             copy.start()
     late = (h * 128 + (lax.broadcasted_iota(jnp.int32, (96, 1024), 1) & 127)) >= bound
     bias = jnp.where(late & (lax.broadcasted_iota(jnp.int32, (96, 1024), 0) == 0), -1e30, 0.0).astype(bf)
+    for name in ("kup", "vup", "cot", "gain2"):
+        small_copy(r, name).wait()
     for g in range(2):
-        kt = r.kup[g].T
-        r.kt[g] = kt
+        r.kt[g] = r.kup[g].T
         r.vt[g] = r.vup[g].T
         at, rope = (0, 256) if g == 0 else (128, 0)
         r.qxt[g, rope + 32 : rope + 128] = bias
@@ -295,6 +309,7 @@
         each(j, grad_gate, grad_up, act)
 
     r.output[...] = r.grad_input[...].astype(bf)
+    result_copy(r, "output").start()
     up = r.g_acc[...]
     mid = r.mid[...]
     inverse = lax.rsqrt(jnp.mean(mid * mid, -1, keepdims=True) + EPS)
@@ -307,10 +322,9 @@
 
 
 RING = 4
-ORDERS = (("y", "z", "x"), ("z", "x", "y"), ("x", "y", "z"))
-JOBS = 16
+ORDERS = (("y", "z", "x"), ("z", "y", "x"), ("x", "y", "z"))
+JOBS = 17
 FEED, OUT, ONE = 0, 1, 2
-PHASES = ("a", "b", "c", "d", "e", "f")
 
 
 def beside(at, axis, step):
@@ -378,83 +392,47 @@
     dense_copy(r, me, which).start()
 
 
-def message(r, me, order, phase, way, job):
-    slot = job % RING
-    kind = PHASES[phase]
+def part_copy(r, me, order, way, job, whole):
+    slot, kind = job % RING, "b" if whole else "a"
     return remote(
         getattr(r, "s" + kind).at[order, slot, way],
         getattr(r, "r" + kind).at[order, slot, way],
-        r.sum_send.at[order, phase, way, slot],
-        r.sum_recv.at[order, phase, way, slot],
-        beside(me, ORDERS[order][phase // 2], 1 if way == 0 else -1),
+        r.part_send.at[order, int(whole), way, slot],
+        r.part_recv.at[order, int(whole), way, slot],
+        beside(me, ORDERS[order][0], 1 if way == 0 else -1),
     )
 
 
-def first_half(r, me, order, stage, job, block):
-    phase = stage * 2
-
-    @pl.when(job >= RING)
-    def _():
-        for way in (0, 1):
-            message(r, me, order, phase, way, job - RING).wait_send()
-
-    ref = getattr(r, "s" + PHASES[phase])
-    for way in (0, 1):
-        half = block[:, way * (W // 2) : (way + 1) * (W // 2)]
-        ref[order, job % RING, way] = half.astype(ref.dtype)
-        message(r, me, order, phase, way, job).start()
-
-
-def second_half(r, me, order, stage, job, block_of):
-    phase = stage * 2 + 1
-
-    @pl.when(job >= RING)
-    def _():
-        for way in (0, 1):
-            message(r, me, order, phase, way, job - RING).wait_send()
-
-    ref, got = getattr(r, "s" + PHASES[phase]), getattr(r, "r" + PHASES[phase - 1])
+def direct_copy(r, me, order, stage, k, job):
+    slot, kind = job % RING, "c" if stage == 1 else "d"
+    return remote(
+        getattr(r, "s" + kind).at[order, slot, k - 1],
+        getattr(r, "r" + kind).at[order, slot, k - 1],
+        r.direct_send.at[order, stage - 1, k - 1, slot],
+        r.direct_recv.at[order, stage - 1, k - 1, slot],
+        beside(me, ORDERS[order][stage], k),
+    )
+
+
+def sends_of(r, me, k, job, orders):
+    for order in orders:
+        if k < 2:
+            for way in (0, 1):
+                yield part_copy(r, me, order, way, job, k == 1)
+        else:
+            for step in (1, 2, 3):
+                yield direct_copy(r, me, order, k - 1, step, job)
+
+
+def products(r, me, job, orders):
     slot = job % RING
-    for way in (0, 1):
-        message(r, me, order, phase - 1, way, job).wait_recv()
-        block = block_of(1 if way == 0 else -1)
-        here = slice(way * (W // 2), (way + 1) * (W // 2))
-        there = slice((1 - way) * (W // 2), (2 - way) * (W // 2))
-        ref[order, slot, way, :, here] = (block[:, here] + got[order, slot, way].astype(f32)).astype(ref.dtype)
-        ref[order, slot, way, :, there] = block[:, there].astype(ref.dtype)
-        message(r, me, order, phase, way, job).start()
-
-
-def total(r, me, order, stage, job, block):
-    phase = stage * 2 + 1
-    got = getattr(r, "r" + PHASES[phase])
-    for way in (0, 1):
-        message(r, me, order, phase, way, job).wait_recv()
-        block = block + got[order, job % RING, way].astype(f32)
-    return block
-
-
-def block_of(r, me, order, stage, job):
-    axis = ORDERS[order][stage]
-    slot = job % RING
-
-    def get(step):
-        index = (me[axis] + step) % 4
-        if stage == 0:
-            return r.d[order, slot, lanes(index * 128, 128), :].astype(f32)
-        if stage == 1:
-            return r.s1[order, slot, lanes(index * 32, 32), :]
-        return r.s2[order, slot, lanes(index * 8, 8), :]
-
-    return get
-
-
-def products(r, me, order, job):
-    slot = job % RING
-
-    def plain(which):
-        g_copy(r, me, order, job).wait_recv()
-        r.d[order, slot] = dot(r.at[order, which], r.g[order, job]).astype(bf)
+
+    def plain(which, orders):
+        for order in orders:
+            g_copy(r, me, order, job).wait_recv()
+        blocks = [dot(r.at[order, which], r.g[order, job]) for order in orders]
+        for order, block in zip(orders, blocks):
+            r.d[order, slot] = block.astype(bf)
 
     def thick(which):
         dense_copy(r, me, which).wait_recv()
@@ -463,54 +441,106 @@
         if which < 2:
             row = ((row >> 2) & 1) * 64 + (row >> 3) * 4 + (row & 3)
         pick = (row == column).astype(bf)
+        blocks = [dot(pick, r.dense[which, q]) for q in range(4)]
         for q in range(4):
-            r.d[order, slot, q * 128 : (q + 1) * 128] = dot(pick, r.dense[which, q]).astype(bf)
-
-    if order == 0:
-        pl.when(job < 11)(lambda: plain(FEED))
-        pl.when(job == 11)(lambda: thick(0))
-        pl.when(job == 12)(lambda: thick(1))
-        pl.when((job == 13) | (job == 14))(lambda: plain(ONE))
-        pl.when(job == 15)(lambda: thick(2))
+            r.d[0, slot, q * 128 : (q + 1) * 128] = blocks[q].astype(bf)
+
+    if len(orders) == 1:
+        thick(2)
+        return
+    pl.when(job < 11)(lambda: plain(FEED, (0, 1, 2)))
+    pl.when((job == 13) | (job == 14))(lambda: plain(ONE, (0, 1, 2)))
+    for number, kind, others in ((11, 0, OUT), (12, 1, OUT)):
+        @pl.when(job == number)
+        def _():
+            thick(kind)
+            plain(others, (1, 2))
+
+    pl.when(job == 15)(lambda: plain(ONE, (1, 2)))
+
+
+def rows_from(ref, index, count):
+    return ref[lanes(index * count, count), :]
+
+
+def sum_step(r, me, k, job, orders):
+    slot = job % RING
+    if k == 0:
+        products(r, me, job, orders)
+    if k < 4:
+        @pl.when(job >= RING)
+        def _():
+            for copy in sends_of(r, me, k, job - RING, orders):
+                copy.wait_send()
+
+    if k:
+        for copy in sends_of(r, me, k - 1, job, orders):
+            copy.wait_recv()
+    place_of = [[me[axis] for axis in ORDERS[order]] for order in range(3)]
+    if k == 0:
+        for order in orders:
+            opposite = rows_from(r.d.at[order, slot], (place_of[order][0] + 2) % 4, 128)
+            for way in (0, 1):
+                r.sa[order, slot, way] = opposite[:, way * (W // 2) : (way + 1) * (W // 2)]
+    elif k == 1:
+        for order in orders:
+            for way in (0, 1):
+                block = rows_from(r.d.at[order, slot], (place_of[order][0] + (1 if way == 0 else 3)) % 4, 128)
+                here = slice(way * (W // 2), (way + 1) * (W // 2))
+                there = slice((1 - way) * (W // 2), (2 - way) * (W // 2))
+                r.sb[order, slot, way, :, here] = (block[:, here].astype(f32) + r.ra[order, slot, way].astype(f32)).astype(bf)
+                r.sb[order, slot, way, :, there] = block[:, there]
+    elif k == 2:
+        for order in orders:
+            own = rows_from(r.d.at[order, slot], place_of[order][0], 128).astype(f32)
+            r.s1[order] = own + r.rb[order, slot, 0].astype(f32) + r.rb[order, slot, 1].astype(f32)
+        for order in orders:
+            for step in (1, 2, 3):
+                r.sc[order, slot, step - 1] = rows_from(r.s1.at[order], (place_of[order][1] + step) % 4, 32).astype(bf)
+            r.own1[order, slot] = rows_from(r.s1.at[order], place_of[order][1], 32)
+    elif k == 3:
+        for order in orders:
+            block = r.own1[order, slot]
+            for step in range(3):
+                block = block + r.rc[order, slot, step].astype(f32)
+            r.s2[order] = block
+        for order in orders:
+            for step in (1, 2, 3):
+                block = rows_from(r.s2.at[order], (place_of[order][2] + step) % 4, 8)
+                r.sd[order, slot, step - 1] = jnp.concatenate([block[:, : W // 2], block[:, W // 2 :]], 0).astype(bf)
+            r.own2[order, slot] = rows_from(r.s2.at[order], place_of[order][2], 8)
     else:
-        plain(jnp.where(job < 11, FEED, jnp.where(job < 13, OUT, ONE)))
-
-
-def sum_step(r, me, order, k, job):
-    get = block_of(r, me, order, min(k // 2, 2), job)
-    if k == 0:
-        products(r, me, order, job)
-        first_half(r, me, order, 0, job, get(2))
-    elif k % 2:
-        second_half(r, me, order, k // 2, job, get)
-    elif k == 2:
-        r.s1[order, job % RING] = total(r, me, order, 0, job, block_of(r, me, order, 0, job)(0))
-        first_half(r, me, order, 1, job, get(2))
-    elif k == 4:
-        r.s2[order, job % RING] = total(r, me, order, 1, job, block_of(r, me, order, 1, job)(0))
-        first_half(r, me, order, 2, job, get(2))
-    else:
-        own = block_of(r, me, order, 2, job)(0)
-        r.sums[order, :, lanes(job * W, W)] = total(r, me, order, 2, job, own)
+        for order in orders:
+            block = r.own2[order, slot]
+            for step in range(3):
+                got = r.rd[order, slot, step].astype(f32)
+                block = block + jnp.concatenate([got[:8], got[8:]], 1)
+            r.sums[order, :, lanes(job * W, W)] = block
+    if k < 4:
+        for copy in sends_of(r, me, k, job, orders):
+            copy.start()
 
 
 def sum_slot(r, me, t):
-    for k in reversed(range(7)):
+    for k in reversed(range(5)):
         job = t - 2 * k
 
-        @pl.when((job >= 0) & (job < JOBS))
-        def _():
-            for order in range(3):
-                sum_step(r, me, order, k, job)
+        @pl.when((job >= 0) & (job < JOBS - 1))
+        def _():
+            sum_step(r, me, k, job, (0, 1, 2))
+
+        @pl.when(job == JOBS - 1)
+        def _():
+            sum_step(r, me, k, job, (0,))
 
 
 def sum_end(r, me):
+    for k in range(4):
+        for back in range(RING):
+            for copy in (*sends_of(r, me, k, JOBS - 1 - back, (0,)), *sends_of(r, me, k, JOBS - 2 - back, (1, 2))):
+                copy.wait_send()
     for order in range(3):
-        for phase in range(6):
-            for way in (0, 1):
-                for job in range(JOBS - RING, JOBS):
-                    message(r, me, order, phase, way, job).wait_send()
-        for job in range(JOBS):
+        for job in range(16):
             if order or job < 11 or job in (13, 14):
                 g_copy(r, me, order, job).wait_send()
         for which in (FEED, OUT, ONE):
@@ -712,6 +742,7 @@
     r.gains[0:1] = jnp.sum(grad * x * inverse, 0, keepdims=True)
     scaled = grad * r.gain1[...].astype(f32)[None]
     r.grad_input[...] = r.mid[...] + inverse * scaled - x * (inverse * inverse * inverse) * jnp.mean(x * scaled, -1, keepdims=True)
+    result_copy(r, "grad_input").start()
 
 
 def finish_rope(r, me):
@@ -735,13 +766,18 @@
     dense_copy(r, me, 2).start()
 
 
-INPUTS = ("x", "cot", "second", "gain1", "gain2", "wkr", "kup", "vup", "wq", "wqr", "wl", "wo_hbm", "wg", "wu", "wd")
+RESULTS = ("output", "grad_input", "sums")
+SMALL = ("x", "gain1", "wkr", "kup", "vup", "cot", "gain2")
+INPUTS = tuple(n + "_hbm" for n in SMALL) + ("second", "wq", "wqr", "wl", "wo_hbm", "wg", "wu", "wd")
 
 
 def scratch():
     vm = lambda *shape, kind=bf: pltpu.VMEM(shape, kind)
     dma = pltpu.SemaphoreType.DMA
     return dict(
+        x=vm(128, 1024), gain1=vm(1024), wkr=vm(32, 1024), kup=vm(2, 256, 512), vup=vm(2, 256, 512), cot=vm(128, 1024), gain2=vm(1024),
+        output=vm(128, 1024), grad_input=vm(128, 1024, kind=f32), sums=vm(3, 8, JOBS * W, kind=f32),
+        small_sem=dma((len(SMALL),)), result_sem=dma((3,)),
         pool=vm(4, 1024, 512), wdpool=vm(4, 256, 1024), wo=vm(1024, 1024),
         first_sem=dma((5,)), chunk_sem=dma((4, 3)),
         n1=vm(128, 1024), n2=vm(128, 1024), gb=vm(128, 1024), ga=vm(1024, 128), attt=vm(1024, 128),
@@ -758,16 +794,17 @@
         in_send=dma((4, 2, 2)), in_z_recv=dma((3, 4)), in_x_recv=dma((3, 4)), out_send=dma((2, 4)), end_recv=dma((2, 3)),
         gkr=vm(128, 128),
         at=vm(3, 3, 512, 256), at_send=vm(3, 3, 512, 128), at_sem=dma((2, 3, 3)),
-        g=vm(3, JOBS, 256, W), g_send=dma((3, JOBS)), g_recv=dma((3, JOBS)),
+        g=vm(3, 16, 256, W), g_send=dma((3, 16)), g_recv=dma((3, 16)),
         dense=vm(3, 4, 256, W), dense_send=vm(3, 4, 128, W), dense_sem=dma((2, 3)),
-        d=vm(3, RING, 512, W), s1=vm(3, RING, 128, W, kind=f32), s2=vm(3, RING, 32, W, kind=f32),
-        sum_send=dma((3, 6, 2, RING)), sum_recv=dma((3, 6, 2, RING)),
+        d=vm(3, RING, 512, W), s1=vm(3, 128, W, kind=f32), s2=vm(3, 32, W, kind=f32),
+        own1=vm(3, RING, 32, W, kind=f32), own2=vm(3, RING, 8, W, kind=f32),
+        part_send=dma((3, 2, 2, RING)), part_recv=dma((3, 2, 2, RING)),
+        direct_send=dma((3, 2, 3, RING)), direct_recv=dma((3, 2, 3, RING)),
         **{
-            side + name: vm(3, RING, 2, rows, width, kind=kind)
+            side + name: vm(3, RING, *shape, kind=kind)
             for side in "sr"
-            for name, rows, width, kind in (
-                ("a", 128, W // 2, bf), ("b", 128, W, bf), ("c", 32, W // 2, bf),
-                ("d", 32, W, bf), ("e", 8, W // 2, f32), ("f", 8, W, f32),
+            for name, shape, kind in (
+                ("a", (2, 128, W // 2), bf), ("b", (2, 128, W), bf), ("c", (3, 32, W), bf), ("d", (3, 16, W // 2), bf),
             )
         },
     )
@@ -779,7 +816,7 @@
     me = place()
     load_first(r)
     barrier = pltpu.get_barrier_semaphore()
-    peers = [(seq, (h + k) % 16) for k in range(1, 16)] + [other_core(me), beside(me, "y", 1), beside(me, "y", -1)]
+    peers = [(seq, (h + k) % 16) for k in range(1, 16)] + [other_core(me), beside(me, "y", 1), beside(me, "y", 2), beside(me, "y", 3)]
     for peer in peers:
         pl.semaphore_signal(barrier, inc=1, device_id=peer, device_id_type=MESH)
     pl.semaphore_wait(barrier, len(peers))
@@ -804,13 +841,13 @@
         for order, value in enumerate((grad_gate, grad_up, act)):
             give(r, me, order, j, value)
 
-        @pl.when(j % 2 == 1)
-        def _():
-            @pl.when(j == 1)
-            def _():
-                wait_rows(r, me, FEED)
-
-            sum_slot(r, me, j // 2)
+        @pl.when(j == 1)
+        def _():
+            wait_rows(r, me, FEED)
+
+        @pl.when((j == 1) | (j == 3) | (j == 5) | (j == 7) | (j == 9) | (j == 10))
+        def _():
+            sum_slot(r, me, sum(jnp.where(j > c, 1, 0) for c in (1, 3, 5, 7, 9, 10,)))
 
     feed(r, begin, each)
     load_first(r, again=True)
@@ -827,47 +864,50 @@
         def _():
             back_step(r, seq, h, b)
 
-        @pl.when(b < 7)
-        def _():
-            sum_slot(r, me, 5 + b)
+        @pl.when((b == 1) | (b == 3) | (b == 5) | (b == 6))
+        def _():
+            sum_slot(r, me, 6 + sum(jnp.where(b > c, 1, 0) for c in (1, 3, 5, 6,)))
 
     finish_queries(r, me)
     wait_rows(r, me, ONE)
+    sum_slot(r, me, 10)
+    sum_slot(r, me, 11)
+    sum_latents(r, seq, h)
     sum_slot(r, me, 12)
-    sum_latents(r, seq, h)
     sum_slot(r, me, 13)
     sum_slot(r, me, 14)
     finish_latent(r, me, seq, h)
+    sum_slot(r, me, 15)
     for i in range(4):
         wait_first(r, i)
     finish_input(r)
     finish_rope(r, me)
 
-    @pl.loop(15, 28)
+    @pl.loop(16, 25)
     def _(t):
         sum_slot(r, me, t)
 
+    result_copy(r, "sums").start()
     sum_end(r, me)
     back_sent(r, seq, h)
     latents_sent(r, seq, h)
     gather_sent(r, seq, h)
+    for name in RESULTS:
+        result_copy(r, name).wait()
 
 
 def run(layer_input, second_start, mixer_gain, w_query, w_query_rope, w_latent, w_key_rope, w_key_up, w_value_up, w_out, feed_gain, w_gate, w_up, w_down, cotangent):
-    args = dict(x=layer_input, cot=cotangent, second=second_start, gain1=mixer_gain, gain2=feed_gain,
-        wkr=w_key_rope.T, kup=w_key_up, vup=w_value_up, wq=w_query, wqr=w_query_rope, wl=w_latent, wo_hbm=w_out, wg=w_gate, wu=w_up, wd=w_down)
-    V, A, S = (pl.BlockSpec(memory_space=m) for m in (pltpu.VMEM, pl.ANY, pltpu.SMEM))
-    specs = {n: V for n in INPUTS}
-    specs["second"] = S
-    for n in ("wq", "wqr", "wl", "wo_hbm", "wg", "wu", "wd"):
-        specs[n] = A
-    outs = dict(output=((128, 1024), bf), grad_input=((128, 1024), f32), sums=((3, 8, JOBS * W), f32))
+    args = dict(x_hbm=layer_input, cot_hbm=cotangent, second=second_start, gain1_hbm=mixer_gain, gain2_hbm=feed_gain,
+        wkr_hbm=w_key_rope.T, kup_hbm=w_key_up, vup_hbm=w_value_up, wq=w_query, wqr=w_query_rope, wl=w_latent, wo_hbm=w_out, wg=w_gate, wu=w_up, wd=w_down)
+    A, S = (pl.BlockSpec(memory_space=m) for m in (pl.ANY, pltpu.SMEM))
+    specs = {n: S if n == "second" else A for n in INPUTS}
+    outs = dict(output_hbm=((128, 1024), bf), grad_input_hbm=((128, 1024), f32), sums_hbm=((3, 8, JOBS * W), f32))
     sc = scratch()
     names = INPUTS + tuple(outs) + tuple(sc)
     output, grad_input, sums = pl.pallas_call(
         lambda *refs: kernel(names, *refs),
         out_shape=[jax.ShapeDtypeStruct(*o) for o in outs.values()],
-        in_specs=[specs[n] for n in INPUTS], out_specs=[V] * len(outs),
+        in_specs=[specs[n] for n in INPUTS], out_specs=[A] * len(outs),
         scratch_shapes=list(sc.values()),
         compiler_params=pltpu.CompilerParams(collective_id=0, has_side_effects=True, vmem_limit_bytes=66900000),
         name="layer",
@@ -880,7 +920,7 @@
     first, second, third = (sums.at[i] for i in range(3))
     outs[0][...] = output[...]
     outs[1][...] = grad_input[...]
-    rope = first[:, 3840:3968]
+    rope = first[:, 4096:4224]
     turned = jnp.concatenate([rope, jnp.zeros((120, 128), f32)], 0).T
     outs[2][...] = turned[32:33, 0:8]
     outs[3][:, 0:512] = second[:, 3328:3840]

time: 131 us -> 128 us (0.977)
  Pallas kernels: 130 us -> 127 us
    pallas_call x1, Pallas kernels: 127 us -> 124 us  [run(): pl.pallas_call(lambda *refs: kernel(names, *refs), out_shape=[jax.ShapeDt...]
where the time goes in v4:
time: 128 us
  Pallas kernels  127 us (99%)
  between operations  1.43 us (1%)
    pallas_call x1, Pallas kernels, run(): pl.pallas_call(lambda *refs: kernel(names, *refs), out_shape=[jax.ShapeDt...  124 us

profile of v4, /device:TPU:0, one launch (start us, length us, event | category | flops | bytes accessed | tf_op | source)
XLA Modules:
  0.0 128.2 jit_solution(16478239449313578686)
XLA Ops:
  1.3 124.4 %layer.1 = (bf16[128,1024]{1,0:T(8,128)(2,1)}, f32[128,1024]{1,0:T(8,128)}, f32[3,8,4352]{2,1,0:T(8,128)}) custom-call(bf16[128,1024]{1,0:T(8,128)(2,1)} %refs_0_.1, bf16[1024]{0:T(1024)(128)(2,1)} %refs_1_.1, bf16[32,1024]{1,0:T(8,128)(2,1)} %bitcast.6, bf16[2,256,512]{2,1,0:T(8,128)(2,1)} %refs_3_.1, bf16[2,256,512]{2,1,0:T(8,128)(2,1)} %refs_4_.1, ...), custom_call_target="tpu_custom_call" | custom-call | tf_op jit(solution)/shard_map/layer/pallas_call | solution.py:907
  125.7 2.3 %place.1 = (bf16[128,1024]{1,0:T(8,128)(2,1)}, f32[128,1024]{1,0:T(8,128)}, f32[1,8]{1,0:T(1,128)}, f32[8,1024]{1,0:T(8,128)}, f32[8,512]{1,0:T(8,128)}, /*index...) custom-call(bf16[128,1024]{1,0:T(8,128)(2,1)} %get-tuple-element.31., ...), custom_call_target="tpu_custom_call" | custom-call | tf_op jit(solution)/shard_map/place/pallas_call | solution.py:945

commit v5 on v4

--- a/solution.py
+++ b/solution.py
@@ -15,7 +15,7 @@
 RATES = [float(v) for v in 10000.0 ** (-np.arange(16) * 2.0 / 32)]
 SCALE = 1.0 / math.sqrt(96)
 DEPTH = 4
-FEATURES, SPLIT = 560, 288
+FEATURES, SPLIT = 560, 256
 
 
 def dot(a, b, ca=1, cb=0):

time: 128 us -> 128 us (level)
  no operation moved by 1% of the time
where the time goes in v5:
time: 128 us
  Pallas kernels  127 us (99%)
  between operations  1.43 us (1%)
    pallas_call x1, Pallas kernels, run(): pl.pallas_call(lambda *refs: kernel(names, *refs), out_shape=[jax.ShapeDt...  125 us

profile of v5, /device:TPU:0, one launch (start us, length us, event | category | flops | bytes accessed | tf_op | source)
XLA Modules:
  0.0 128.3 jit_solution(16681364003549102135)
XLA Ops:
  1.3 124.5 %layer.1 = (bf16[128,1024]{1,0:T(8,128)(2,1)}, f32[128,1024]{1,0:T(8,128)}, f32[3,8,4352]{2,1,0:T(8,128)}) custom-call(bf16[128,1024]{1,0:T(8,128)(2,1)} %refs_0_.1, bf16[1024]{0:T(1024)(128)(2,1)} %refs_1_.1, bf16[32,1024]{1,0:T(8,128)(2,1)} %bitcast.6, bf16[2,256,512]{2,1,0:T(8,128)(2,1)} %refs_3_.1, bf16[2,256,512]{2,1,0:T(8,128)(2,1)} %refs_4_.1, ...), custom_call_target="tpu_custom_call" | custom-call | tf_op jit(solution)/shard_map/layer/pallas_call | solution.py:907
  125.9 2.3 %place.1 = (bf16[128,1024]{1,0:T(8,128)(2,1)}, f32[128,1024]{1,0:T(8,128)}, f32[1,8]{1,0:T(1,128)}, f32[8,1024]{1,0:T(8,128)}, f32[8,512]{1,0:T(8,128)}, /*index...) custom-call(bf16[128,1024]{1,0:T(8,128)(2,1)} %get-tuple-element.31., ...), custom_call_target="tpu_custom_call" | custom-call | tf_op jit(solution)/shard_map/place/pallas_call | solution.py:945
